TPU v7x, 512 devices: a whole 4x4x16 slice. The times are simulated.
512 devices in a mesh: leaf: 512 (over y, z, x, core).
Axes of the slice: x: 4, y: 4, z: 16, core: 2. Of those that a mesh axis runs over, the one named last changes fastest.
Arguments:
- right_side: float32 [131072, 128], P('leaf'), may hold values from -6 to 6
- leaf_inverse: float32 [131072, 256], P('leaf'), may hold values from -1 to 3, as said below
- bases: float32 [9, 131072, 128], P(None, 'leaf'), may hold values from -5 to 5
Outputs:
- solution: float32 [131072, 128], P('leaf')
Inputs may be any that keep to these rules, and one draw needn't show every extreme that they name: `leaf_inverse`: each leaf's block is a symmetric matrix with a positive diagonal; for every node and level, the singular values of I - G_o G_w lie between 0.5 and 1.5.
All inputs are finite; a program needn't handle non-finite values.
Results may differ from a plain program's by a relative error of at most 0.0001.
Values sent between devices are 32-bit elements; how exact they have to be, the bound alone decides.
A program may use at most 128 MiB of HBM per device.

v0:
```python
import jax
import jax.numpy as jnp
from jax import lax
from jax.sharding import PartitionSpec as P

HIGH = lax.Precision.HIGHEST


def swapped(value, axis, bit):
    mask = 2**bit
    pairs = [(source, source ^ mask) for source in range(lax.axis_size(axis))]
    return lax.ppermute(value, axis, pairs)


def core_solve(own_half, sibling_half):
    basis_rank = own_half.shape[0]
    g_own = own_half[:, -basis_rank:]
    s_own = own_half[:, :-basis_rank]
    g_other = sibling_half[:, -basis_rank:]
    s_other = sibling_half[:, :-basis_rank]
    system = jnp.eye(basis_rank, dtype=jnp.float32) - jnp.dot(
        g_other, g_own, precision=HIGH, preferred_element_type=jnp.float32
    )
    right_part = s_other - jnp.dot(
        g_other, s_own, precision=HIGH, preferred_element_type=jnp.float32
    )
    normal = jnp.dot(system.T, system, precision=HIGH, preferred_element_type=jnp.float32)
    factor = jnp.linalg.cholesky(normal)
    return jax.scipy.linalg.cho_solve(
        (factor, True),
        jnp.dot(system.T, right_part, precision=HIGH, preferred_element_type=jnp.float32),
    )


def half_sums(projected, tree_level):
    running = projected
    for bit_index in range(tree_level - 1):
        running = running + swapped(running, "leaf", bit_index)
    sibling_half = swapped(running, "leaf", tree_level - 1)
    return (running, sibling_half)


def shards(right_side, leaf_inverse, bases):
    tree_depth = bases.shape[0]
    basis_rank = bases.shape[2]
    stacked = jnp.concatenate(
        [right_side] + [bases[index_level] for index_level in reversed(range(tree_depth))], axis=1
    )
    current = jnp.dot(leaf_inverse, stacked, precision=HIGH, preferred_element_type=jnp.float32)
    for tree_level in range(1, tree_depth + 1):
        active_cols = current.shape[1]
        level_basis = bases[tree_level - 1]
        projected = jnp.dot(
            level_basis.T, current, precision=HIGH, preferred_element_type=jnp.float32
        )
        own_half, sibling_half = half_sums(projected, tree_level)
        weights = core_solve(own_half, sibling_half)
        corrected = current[:, active_cols - basis_rank :]
        current = current[:, : active_cols - basis_rank] - jnp.dot(
            corrected, weights, precision=HIGH, preferred_element_type=jnp.float32
        )
    return current


def solution(mesh):
    return jax.shard_map(
        shards,
        mesh=mesh,
        in_specs=(P("leaf", None), P("leaf", None), P(None, "leaf", None)),
        out_specs=P("leaf", None),
        check_vma=False,
    )
```

profile of v0, /device:TPU:1, one launch (start us, length us, event | category | flops | bytes accessed | tf_op | source)
XLA Modules:
  0.0 803.4 jit_solution(8865503041472832340)
XLA Ops:
  8.3 9.0 %collective-permute-start = (f32[128,1280]{0,1:T(8,128)S(1)}, f32[128,1280]{0,1:T(8,128)S(1)}, u32[]{:S(2)}, u32[]{:S(2)}) collective-permute-start(f32[128,1280]{0,1:T(8,128)S(1)} %convolution_bitcast_fusion.1), channel_id=1, source_target_pairs={{0,1},{1,0},{2,3},{3,2},{4,5},{5,4},{6,7},{7,6},{8,9},{9,8},{10,11... | collective-permute-start | bytes 1966088 | tf_op jit(solution)/shard_map/ppermute | solution.py:12
  19.4 11.7 %cholesky.149 = f32[128,128]{1,0:T(8,128)S(1)} custom-call(f32[128,128]{1,0:T(8,128)S(1)} %fusion.116), custom_call_target="Cholesky" | custom-call | tf_op jit(solution)/shard_map/jit(cholesky)/cholesky | solution.py:28
  32.5 9.8 %custom-call.65 = f32[1,128,128]{1,2,0:T(8,128)S(1)} custom-call(f32[1,128,128]{2,1,0:T(8,128)S(1)} %fusion.51), custom_call_target="InvertDiagBlocksLowerTriangular" | custom-call | tf_op jit(solution)/shard_map/jit(_cho_solve)/triangular_solve | solution.py:29
  54.4 14.1 %collective-permute-done.2 = f32[128,1152]{0,1:T(8,128)S(1)} collective-permute-done((f32[128,1152]{0,1:T(8,128)S(1)}, f32[128,1152]{0,1:T(8,128)S(1)}, u32[]{:S(2)}, u32[]{:S(2)}) %collective-permute-start.2) | collective-permute-done | bytes 589856 | tf_op jit(solution)/shard_map/ppermute | solution.py:12
  69.2 11.7 %cholesky.160 = f32[128,128]{1,0:T(8,128)S(1)} custom-call(f32[128,128]{1,0:T(8,128)S(1)} %fusion.111), custom_call_target="Cholesky" | custom-call | tf_op jit(solution)/shard_map/jit(cholesky)/cholesky | solution.py:28
  82.3 9.8 %custom-call.66 = f32[1,128,128]{1,2,0:T(8,128)S(1)} custom-call(f32[1,128,128]{2,1,0:T(8,128)S(1)} %fusion.52), custom_call_target="InvertDiagBlocksLowerTriangular" | custom-call | tf_op jit(solution)/shard_map/jit(_cho_solve)/triangular_solve | solution.py:29
  104.1 13.1 %collective-permute-done.4 = f32[128,1024]{0,1:T(8,128)S(1)} collective-permute-done((f32[128,1024]{0,1:T(8,128)S(1)}, f32[128,1024]{0,1:T(8,128)S(1)}, u32[]{:S(2)}, u32[]{:S(2)}) %collective-permute-start.4) | collective-permute-done | bytes 524320 | tf_op jit(solution)/shard_map/ppermute | solution.py:12
  119.4 13.5 %collective-permute-done.5 = f32[128,1024]{0,1:T(8,128)S(1)} collective-permute-done((f32[128,1024]{0,1:T(8,128)S(1)}, f32[128,1024]{0,1:T(8,128)S(1)}, u32[]{:S(2)}, u32[]{:S(2)}) %collective-permute-start.5) | collective-permute-done | bytes 524320 | tf_op jit(solution)/shard_map/ppermute | solution.py:12
  133.6 11.7 %cholesky.171 = f32[128,128]{1,0:T(8,128)S(1)} custom-call(f32[128,128]{1,0:T(8,128)S(1)} %fusion.106), custom_call_target="Cholesky" | custom-call | tf_op jit(solution)/shard_map/jit(cholesky)/cholesky | solution.py:28
  146.6 9.8 %custom-call.67 = f32[1,128,128]{1,2,0:T(8,128)S(1)} custom-call(f32[1,128,128]{2,1,0:T(8,128)S(1)} %fusion.53), custom_call_target="InvertDiagBlocksLowerTriangular" | custom-call | tf_op jit(solution)/shard_map/jit(_cho_solve)/triangular_solve | solution.py:29
  168.0 11.7 %collective-permute-done.7 = f32[128,896]{0,1:T(8,128)S(1)} collective-permute-done((f32[128,896]{0,1:T(8,128)S(1)}, f32[128,896]{0,1:T(8,128)S(1)}, u32[]{:S(2)}, u32[]{:S(2)}) %collective-permute-start.7) | collective-permute-done | bytes 458784 | tf_op jit(solution)/shard_map/ppermute | solution.py:12
  181.7 12.3 %collective-permute-done.8 = f32[128,896]{0,1:T(8,128)S(1)} collective-permute-done((f32[128,896]{0,1:T(8,128)S(1)}, f32[128,896]{0,1:T(8,128)S(1)}, u32[]{:S(2)}, u32[]{:S(2)}) %collective-permute-start.8) | collective-permute-done | bytes 458784 | tf_op jit(solution)/shard_map/ppermute | solution.py:12
  196.2 9.7 %collective-permute-done.9 = f32[128,896]{0,1:T(8,128)} collective-permute-done((f32[128,896]{0,1:T(8,128)S(1)}, f32[128,896]{0,1:T(8,128)}, u32[]{:S(2)}, u32[]{:S(2)}) %collective-permute-start.9) | collective-permute-done | bytes 458784 | tf_op jit(solution)/shard_map/ppermute | solution.py:12
  207.5 11.7 %cholesky.182 = f32[128,128]{1,0:T(8,128)S(1)} custom-call(f32[128,128]{1,0:T(8,128)S(1)} %fusion.101), custom_call_target="Cholesky" | custom-call | tf_op jit(solution)/shard_map/jit(cholesky)/cholesky | solution.py:28
  220.5 9.8 %custom-call.68 = f32[1,128,128]{1,2,0:T(8,128)S(1)} custom-call(f32[1,128,128]{2,1,0:T(8,128)S(1)} %fusion.54), custom_call_target="InvertDiagBlocksLowerTriangular" | custom-call | tf_op jit(solution)/shard_map/jit(_cho_solve)/triangular_solve | solution.py:29
  244.1 10.3 %collective-permute-done.11 = f32[128,768]{0,1:T(8,128)S(1)} collective-permute-done((f32[128,768]{0,1:T(8,128)S(1)}, f32[128,768]{0,1:T(8,128)S(1)}, u32[]{:S(2)}, u32[]{:S(2)}) %collective-permute-start.11) | collective-permute-done | bytes 393248 | tf_op jit(solution)/shard_map/ppermute | solution.py:12
  256.3 10.9 %collective-permute-done.12 = f32[128,768]{0,1:T(8,128)S(1)} collective-permute-done((f32[128,768]{0,1:T(8,128)S(1)}, f32[128,768]{0,1:T(8,128)S(1)}, u32[]{:S(2)}, u32[]{:S(2)}) %collective-permute-start.12) | collective-permute-done | bytes 393248 | tf_op jit(solution)/shard_map/ppermute | solution.py:12
  269.2 8.4 %collective-permute-done.13 = f32[128,768]{0,1:T(8,128)S(1)} collective-permute-done((f32[128,768]{0,1:T(8,128)S(1)}, f32[128,768]{0,1:T(8,128)S(1)}, u32[]{:S(2)}, u32[]{:S(2)}) %collective-permute-start.13) | collective-permute-done | bytes 393248 | tf_op jit(solution)/shard_map/ppermute | solution.py:12
  280.0 19.7 %collective-permute-done.14 = f32[128,768]{0,1:T(8,128)S(1)} collective-permute-done((f32[128,768]{0,1:T(8,128)S(1)}, f32[128,768]{0,1:T(8,128)S(1)}, u32[]{:S(2)}, u32[]{:S(2)}) %collective-permute-start.14) | collective-permute-done | bytes 393248 | tf_op jit(solution)/shard_map/ppermute | solution.py:12
  300.4 11.7 %cholesky.193 = f32[128,128]{1,0:T(8,128)S(1)} custom-call(f32[128,128]{1,0:T(8,128)S(1)} %fusion.96), custom_call_target="Cholesky" | custom-call | tf_op jit(solution)/shard_map/jit(cholesky)/cholesky | solution.py:28
  313.4 9.8 %custom-call.69 = f32[1,128,128]{1,2,0:T(8,128)S(1)} custom-call(f32[1,128,128]{2,1,0:T(8,128)S(1)} %fusion.55), custom_call_target="InvertDiagBlocksLowerTriangular" | custom-call | tf_op jit(solution)/shard_map/jit(_cho_solve)/triangular_solve | solution.py:29
  332.1 8.9 %collective-permute-done.16 = f32[128,640]{0,1:T(8,128)S(1)} collective-permute-done((f32[128,640]{0,1:T(8,128)S(1)}, f32[128,640]{0,1:T(8,128)S(1)}, u32[]{:S(2)}, u32[]{:S(2)}) %collective-permute-start.16) | collective-permute-done | bytes 327712 | tf_op jit(solution)/shard_map/ppermute | solution.py:12
  343.0 9.5 %collective-permute-done.17 = f32[128,640]{0,1:T(8,128)S(1)} collective-permute-done((f32[128,640]{0,1:T(8,128)S(1)}, f32[128,640]{0,1:T(8,128)S(1)}, u32[]{:S(2)}, u32[]{:S(2)}) %collective-permute-start.17) | collective-permute-done | bytes 327712 | tf_op jit(solution)/shard_map/ppermute | solution.py:12
  354.4 7.0 collective-permute-done.18
  363.4 17.5 %collective-permute-done.19 = f32[128,640]{0,1:T(8,128)S(1)} collective-permute-done((f32[128,640]{0,1:T(8,128)S(1)}, f32[128,640]{0,1:T(8,128)S(1)}, u32[]{:S(2)}, u32[]{:S(2)}) %collective-permute-start.19) | collective-permute-done | bytes 327712 | tf_op jit(solution)/shard_map/ppermute | solution.py:12
  384.7 30.1 %collective-permute-done.20 = f32[128,640]{0,1:T(8,128)S(1)} collective-permute-done((f32[128,640]{0,1:T(8,128)S(1)}, f32[128,640]{0,1:T(8,128)S(1)}, u32[]{:S(2)}, u32[]{:S(2)}) %collective-permute-start.20) | collective-permute-done | bytes 327712 | tf_op jit(solution)/shard_map/ppermute | solution.py:12
  415.6 11.7 %cholesky.204 = f32[128,128]{1,0:T(8,128)S(1)} custom-call(f32[128,128]{1,0:T(8,128)S(1)} %fusion.91), custom_call_target="Cholesky" | custom-call | tf_op jit(solution)/shard_map/jit(cholesky)/cholesky | solution.py:28
  428.6 9.8 %custom-call.70 = f32[1,128,128]{1,2,0:T(8,128)S(1)} custom-call(f32[1,128,128]{2,1,0:T(8,128)S(1)} %fusion.56), custom_call_target="InvertDiagBlocksLowerTriangular" | custom-call | tf_op jit(solution)/shard_map/jit(_cho_solve)/triangular_solve | solution.py:29
  448.0 6.3 collective-permute-done.22
  457.8 6.5 collective-permute-done.23
  466.3 5.6 collective-permute-done.24
  473.9 14.3 %collective-permute-done.25 = f32[128,512]{0,1:T(8,128)S(1)} collective-permute-done((f32[128,512]{0,1:T(8,128)S(1)}, f32[128,512]{0,1:T(8,128)S(1)}, u32[]{:S(2)}, u32[]{:S(2)}) %collective-permute-start.25) | collective-permute-done | bytes 262176 | tf_op jit(solution)/shard_map/ppermute | solution.py:12
  490.8 24.7 %collective-permute-done.26 = f32[128,512]{0,1:T(8,128)S(1)} collective-permute-done((f32[128,512]{0,1:T(8,128)S(1)}, f32[128,512]{0,1:T(8,128)S(1)}, u32[]{:S(2)}, u32[]{:S(2)}) %collective-permute-start.26) | collective-permute-done | bytes 262176 | tf_op jit(solution)/shard_map/ppermute | solution.py:12
  515.5 17.3 %collective-permute-start.27 = (f32[128,512]{0,1:T(8,128)S(1)}, f32[128,512]{0,1:T(8,128)S(1)}, u32[]{:S(2)}, u32[]{:S(2)}) collective-permute-start(f32[128,512]{0,1:T(8,128)S(1)} %add.189), channel_id=1, source_target_pairs={{0,64},{1,65},{2,66},{3,67},{4,68},{5,69},{6,70},{7,71},{8,72},{9,... | collective-permute-start | bytes 786440 | tf_op jit(solution)/shard_map/ppermute | solution.py:12
  532.8 16.0 %collective-permute-done.27 = f32[128,512]{0,1:T(8,128)S(1)} collective-permute-done((f32[128,512]{0,1:T(8,128)S(1)}, f32[128,512]{0,1:T(8,128)S(1)}, u32[]{:S(2)}, u32[]{:S(2)}) %collective-permute-start.27) | collective-permute-done | bytes 262176 | tf_op jit(solution)/shard_map/ppermute | solution.py:12
  549.5 11.7 %cholesky.215 = f32[128,128]{1,0:T(8,128)S(1)} custom-call(f32[128,128]{1,0:T(8,128)S(1)} %fusion.86), custom_call_target="Cholesky" | custom-call | tf_op jit(solution)/shard_map/jit(cholesky)/cholesky | solution.py:28
  562.5 9.8 %custom-call.71 = f32[1,128,128]{1,2,0:T(8,128)S(1)} custom-call(f32[1,128,128]{2,1,0:T(8,128)S(1)} %fusion.57), custom_call_target="InvertDiagBlocksLowerTriangular" | custom-call | tf_op jit(solution)/shard_map/jit(_cho_solve)/triangular_solve | solution.py:29
  603.3 10.2 %collective-permute-done.32 = f32[128,384]{0,1:T(8,128)S(1)} collective-permute-done((f32[128,384]{0,1:T(8,128)S(1)}, f32[128,384]{0,1:T(8,128)S(1)}, u32[]{:S(2)}, u32[]{:S(2)}) %collective-permute-start.32) | collective-permute-done | bytes 196640 | tf_op jit(solution)/shard_map/ppermute | solution.py:12
  617.1 18.6 %collective-permute-done.33 = f32[128,384]{0,1:T(8,128)S(1)} collective-permute-done((f32[128,384]{0,1:T(8,128)S(1)}, f32[128,384]{0,1:T(8,128)S(1)}, u32[]{:S(2)}, u32[]{:S(2)}) %collective-permute-start.33) | collective-permute-done | bytes 196640 | tf_op jit(solution)/shard_map/ppermute | solution.py:12
  635.7 8.7 %collective-permute-start.34 = (f32[128,384]{0,1:T(8,128)S(1)}, f32[128,384]{0,1:T(8,128)S(1)}, u32[]{:S(2)}, u32[]{:S(2)}) collective-permute-start(f32[128,384]{0,1:T(8,128)S(1)} %add.195), channel_id=1, source_target_pairs={{0,64},{1,65},{2,66},{3,67},{4,68},{5,69},{6,70},{7,71},{8,72},{9,... | collective-permute-start | bytes 589832 | tf_op jit(solution)/shard_map/ppermute | solution.py:12
  644.4 17.7 %collective-permute-done.34 = f32[128,384]{0,1:T(8,128)S(1)} collective-permute-done((f32[128,384]{0,1:T(8,128)S(1)}, f32[128,384]{0,1:T(8,128)S(1)}, u32[]{:S(2)}, u32[]{:S(2)}) %collective-permute-start.34) | collective-permute-done | bytes 196640 | tf_op jit(solution)/shard_map/ppermute | solution.py:12
  670.7 11.7 %cholesky.226 = f32[128,128]{1,0:T(8,128)S(1)} custom-call(f32[128,128]{1,0:T(8,128)S(1)} %fusion.81), custom_call_target="Cholesky" | custom-call | tf_op jit(solution)/shard_map/jit(cholesky)/cholesky | solution.py:28
  683.8 9.8 %custom-call.72 = f32[1,128,128]{1,2,0:T(8,128)S(1)} custom-call(f32[1,128,128]{2,1,0:T(8,128)S(1)} %fusion.58), custom_call_target="InvertDiagBlocksLowerTriangular" | custom-call | tf_op jit(solution)/shard_map/jit(_cho_solve)/triangular_solve | solution.py:29
  721.3 5.8 collective-permute-done.40
  729.8 15.7 %collective-permute-done.41 = f32[128,256]{0,1:T(8,128)S(1)} collective-permute-done((f32[128,256]{0,1:T(8,128)S(1)}, f32[128,256]{0,1:T(8,128)S(1)}, u32[]{:S(2)}, u32[]{:S(2)}) %collective-permute-start.41) | collective-permute-done | bytes 131104 | tf_op jit(solution)/shard_map/ppermute | solution.py:12
  750.0 13.6 %collective-permute-done.42 = f32[128,256]{0,1:T(8,128)S(1)} collective-permute-done((f32[128,256]{0,1:T(8,128)S(1)}, f32[128,256]{0,1:T(8,128)S(1)}, u32[]{:S(2)}, u32[]{:S(2)}) %collective-permute-start.42) | collective-permute-done | bytes 131104 | tf_op jit(solution)/shard_map/ppermute | solution.py:12
  778.0 11.7 %cholesky.237 = f32[128,128]{1,0:T(8,128)S(1)} custom-call(f32[128,128]{1,0:T(8,128)S(1)} %fusion.76), custom_call_target="Cholesky" | custom-call | tf_op jit(solution)/shard_map/jit(cholesky)/cholesky | solution.py:28
  791.0 9.8 %custom-call.73 = f32[1,128,128]{1,2,0:T(8,128)S(1)} custom-call(f32[1,128,128]{2,1,0:T(8,128)S(1)} %fusion.59), custom_call_target="InvertDiagBlocksLowerTriangular" | custom-call | tf_op jit(solution)/shard_map/jit(_cho_solve)/triangular_solve | solution.py:29
  (231 shorter events, 221.1 us)
Async XLA Ops:
  0.0 4.8 copy-start
  0.0 4.7 copy-start.1
  8.3 10.5 %collective-permute-start = (f32[128,1280]{0,1:T(8,128)S(1)}, f32[128,1280]{0,1:T(8,128)S(1)}, u32[]{:S(2)}, u32[]{:S(2)}) collective-permute-start(f32[128,1280]{0,1:T(8,128)S(1)} %convolution_bitcast_fusion.1), channel_id=1, source_target_pairs={{0,1},{1,0},{2,3},{3,2},{4,5},{5,4},{6,7},{7,6},{8,9},{9,8},{10,11... | collective-permute-start | bytes 1966088 | tf_op jit(solution)/shard_map/ppermute | solution.py:12
  48.1 3.9 collective-permute-start.1
  52.1 16.4 %collective-permute-start.2 = (f32[128,1152]{0,1:T(8,128)S(1)}, f32[128,1152]{0,1:T(8,128)S(1)}, u32[]{:S(2)}, u32[]{:S(2)}) collective-permute-start(f32[128,1152]{0,1:T(8,128)S(1)} %add.169), channel_id=1, source_target_pairs={{0,2},{1,3},{2,0},{3,1},{4,6},{5,7},{6,4},{7,5},{8,10},{9,11},{10,... | collective-permute-start | bytes 1769480 | tf_op jit(solution)/shard_map/ppermute | solution.py:12
  97.5 4.6 collective-permute-start.3
  102.2 15.0 %collective-permute-start.4 = (f32[128,1024]{0,1:T(8,128)S(1)}, f32[128,1024]{0,1:T(8,128)S(1)}, u32[]{:S(2)}, u32[]{:S(2)}) collective-permute-start(f32[128,1024]{0,1:T(8,128)S(1)} %add.170), channel_id=1, source_target_pairs={{0,2},{1,3},{2,0},{3,1},{4,6},{5,7},{6,4},{7,5},{8,10},{9,11},{10,... | collective-permute-start | bytes 1572872 | tf_op jit(solution)/shard_map/ppermute | solution.py:12
  117.3 15.6 %collective-permute-start.5 = (f32[128,1024]{0,1:T(8,128)S(1)}, f32[128,1024]{0,1:T(8,128)S(1)}, u32[]{:S(2)}, u32[]{:S(2)}) collective-permute-start(f32[128,1024]{0,1:T(8,128)S(1)} %add.171), channel_id=1, source_target_pairs={{0,4},{1,5},{2,6},{3,7},{4,0},{5,1},{6,2},{7,3},{8,12},{9,13},{10,... | collective-permute-start | bytes 1572872 | tf_op jit(solution)/shard_map/ppermute | solution.py:12
  158.2 1.5 copy-start.2
  160.6 5.5 collective-permute-start.6
  166.1 13.6 %collective-permute-start.7 = (f32[128,896]{0,1:T(8,128)S(1)}, f32[128,896]{0,1:T(8,128)S(1)}, u32[]{:S(2)}, u32[]{:S(2)}) collective-permute-start(f32[128,896]{0,1:T(8,128)S(1)} %add.172), channel_id=1, source_target_pairs={{0,2},{1,3},{2,0},{3,1},{4,6},{5,7},{6,4},{7,5},{8,10},{9,11},{10,... | collective-permute-start | bytes 1376264 | tf_op jit(solution)/shard_map/ppermute | solution.py:12
  179.8 14.2 %collective-permute-start.8 = (f32[128,896]{0,1:T(8,128)S(1)}, f32[128,896]{0,1:T(8,128)S(1)}, u32[]{:S(2)}, u32[]{:S(2)}) collective-permute-start(f32[128,896]{0,1:T(8,128)S(1)} %add.173), channel_id=1, source_target_pairs={{0,4},{1,5},{2,6},{3,7},{4,0},{5,1},{6,2},{7,3},{8,12},{9,13},{10,... | collective-permute-start | bytes 1376264 | tf_op jit(solution)/shard_map/ppermute | solution.py:12
  194.1 11.9 %collective-permute-start.9 = (f32[128,896]{0,1:T(8,128)S(1)}, f32[128,896]{0,1:T(8,128)}, u32[]{:S(2)}, u32[]{:S(2)}) collective-permute-start(f32[128,896]{0,1:T(8,128)S(1)} %add.174), channel_id=1, source_target_pairs={{0,8},{1,9},{2,10},{3,11},{4,12},{5,13},{6,14},{7,15},{8,0},{9,1},... | collective-permute-start | bytes 1376264 | tf_op jit(solution)/shard_map/ppermute | solution.py:12
  235.8 6.3 collective-permute-start.10
  242.1 12.2 %collective-permute-start.11 = (f32[128,768]{0,1:T(8,128)S(1)}, f32[128,768]{0,1:T(8,128)S(1)}, u32[]{:S(2)}, u32[]{:S(2)}) collective-permute-start(f32[128,768]{0,1:T(8,128)S(1)} %add.175), channel_id=1, source_target_pairs={{0,2},{1,3},{2,0},{3,1},{4,6},{5,7},{6,4},{7,5},{8,10},{9,11},{10,... | collective-permute-start | bytes 1179656 | tf_op jit(solution)/shard_map/ppermute | solution.py:12
  254.4 12.8 %collective-permute-start.12 = (f32[128,768]{0,1:T(8,128)S(1)}, f32[128,768]{0,1:T(8,128)S(1)}, u32[]{:S(2)}, u32[]{:S(2)}) collective-permute-start(f32[128,768]{0,1:T(8,128)S(1)} %add.176), channel_id=1, source_target_pairs={{0,4},{1,5},{2,6},{3,7},{4,0},{5,1},{6,2},{7,3},{8,12},{9,13},{10,... | collective-permute-start | bytes 1179656 | tf_op jit(solution)/shard_map/ppermute | solution.py:12
  267.3 10.4 %collective-permute-start.13 = (f32[128,768]{0,1:T(8,128)S(1)}, f32[128,768]{0,1:T(8,128)S(1)}, u32[]{:S(2)}, u32[]{:S(2)}) collective-permute-start(f32[128,768]{0,1:T(8,128)S(1)} %add.177), channel_id=1, source_target_pairs={{0,8},{1,9},{2,10},{3,11},{4,12},{5,13},{6,14},{7,15},{8,0},{9,1},... | collective-permute-start | bytes 1179656 | tf_op jit(solution)/shard_map/ppermute | solution.py:12
  277.7 22.0 %collective-permute-start.14 = (f32[128,768]{0,1:T(8,128)S(1)}, f32[128,768]{0,1:T(8,128)S(1)}, u32[]{:S(2)}, u32[]{:S(2)}) collective-permute-start(f32[128,768]{0,1:T(8,128)S(1)} %add.178), channel_id=1, source_target_pairs={{0,16},{1,17},{2,18},{3,19},{4,20},{5,21},{6,22},{7,23},{8,24},{9,... | collective-permute-start | bytes 1179656 | tf_op jit(solution)/shard_map/ppermute | solution.py:12
  326.5 3.6 collective-permute-start.15
  330.2 10.8 %collective-permute-start.16 = (f32[128,640]{0,1:T(8,128)S(1)}, f32[128,640]{0,1:T(8,128)S(1)}, u32[]{:S(2)}, u32[]{:S(2)}) collective-permute-start(f32[128,640]{0,1:T(8,128)S(1)} %add.179), channel_id=1, source_target_pairs={{0,2},{1,3},{2,0},{3,1},{4,6},{5,7},{6,4},{7,5},{8,10},{9,11},{10,... | collective-permute-start | bytes 983048 | tf_op jit(solution)/shard_map/ppermute | solution.py:12
  341.0 11.4 %collective-permute-start.17 = (f32[128,640]{0,1:T(8,128)S(1)}, f32[128,640]{0,1:T(8,128)S(1)}, u32[]{:S(2)}, u32[]{:S(2)}) collective-permute-start(f32[128,640]{0,1:T(8,128)S(1)} %add.180), channel_id=1, source_target_pairs={{0,4},{1,5},{2,6},{3,7},{4,0},{5,1},{6,2},{7,3},{8,12},{9,13},{10,... | collective-permute-start | bytes 983048 | tf_op jit(solution)/shard_map/ppermute | solution.py:12
  352.5 9.0 %collective-permute-start.18 = (f32[128,640]{0,1:T(8,128)S(1)}, f32[128,640]{0,1:T(8,128)S(1)}, u32[]{:S(2)}, u32[]{:S(2)}) collective-permute-start(f32[128,640]{0,1:T(8,128)S(1)} %add.181), channel_id=1, source_target_pairs={{0,8},{1,9},{2,10},{3,11},{4,12},{5,13},{6,14},{7,15},{8,0},{9,1},... | collective-permute-start | bytes 983048 | tf_op jit(solution)/shard_map/ppermute | solution.py:12
  361.5 19.4 %collective-permute-start.19 = (f32[128,640]{0,1:T(8,128)S(1)}, f32[128,640]{0,1:T(8,128)S(1)}, u32[]{:S(2)}, u32[]{:S(2)}) collective-permute-start(f32[128,640]{0,1:T(8,128)S(1)} %add.182), channel_id=1, source_target_pairs={{0,16},{1,17},{2,18},{3,19},{4,20},{5,21},{6,22},{7,23},{8,24},{9,... | collective-permute-start | bytes 983048 | tf_op jit(solution)/shard_map/ppermute | solution.py:12
  380.9 33.9 %collective-permute-start.20 = (f32[128,640]{0,1:T(8,128)S(1)}, f32[128,640]{0,1:T(8,128)S(1)}, u32[]{:S(2)}, u32[]{:S(2)}) collective-permute-start(f32[128,640]{0,1:T(8,128)S(1)} %add.183), channel_id=1, source_target_pairs={{0,32},{1,33},{2,34},{3,35},{4,36},{5,37},{6,38},{7,39},{8,40},{9,... | collective-permute-start | bytes 983048 | tf_op jit(solution)/shard_map/ppermute | solution.py:12
  441.3 3.5 collective-permute-start.21
  444.8 9.4 %collective-permute-start.22 = (f32[128,512]{0,1:T(8,128)S(1)}, f32[128,512]{0,1:T(8,128)S(1)}, u32[]{:S(2)}, u32[]{:S(2)}) collective-permute-start(f32[128,512]{0,1:T(8,128)S(1)} %add.184), channel_id=1, source_target_pairs={{0,2},{1,3},{2,0},{3,1},{4,6},{5,7},{6,4},{7,5},{8,10},{9,11},{10,... | collective-permute-start | bytes 786440 | tf_op jit(solution)/shard_map/ppermute | solution.py:12
  454.3 10.0 %collective-permute-start.23 = (f32[128,512]{0,1:T(8,128)S(1)}, f32[128,512]{0,1:T(8,128)S(1)}, u32[]{:S(2)}, u32[]{:S(2)}) collective-permute-start(f32[128,512]{0,1:T(8,128)S(1)} %add.185), channel_id=1, source_target_pairs={{0,4},{1,5},{2,6},{3,7},{4,0},{5,1},{6,2},{7,3},{8,12},{9,13},{10,... | collective-permute-start | bytes 786440 | tf_op jit(solution)/shard_map/ppermute | solution.py:12
  464.3 7.6 collective-permute-start.24
  471.9 16.2 %collective-permute-start.25 = (f32[128,512]{0,1:T(8,128)S(1)}, f32[128,512]{0,1:T(8,128)S(1)}, u32[]{:S(2)}, u32[]{:S(2)}) collective-permute-start(f32[128,512]{0,1:T(8,128)S(1)} %add.187), channel_id=1, source_target_pairs={{0,16},{1,17},{2,18},{3,19},{4,20},{5,21},{6,22},{7,23},{8,24},{9,... | collective-permute-start | bytes 786440 | tf_op jit(solution)/shard_map/ppermute | solution.py:12
  488.2 27.2 %collective-permute-start.26 = (f32[128,512]{0,1:T(8,128)S(1)}, f32[128,512]{0,1:T(8,128)S(1)}, u32[]{:S(2)}, u32[]{:S(2)}) collective-permute-start(f32[128,512]{0,1:T(8,128)S(1)} %add.188), channel_id=1, source_target_pairs={{0,32},{1,33},{2,34},{3,35},{4,36},{5,37},{6,38},{7,39},{8,40},{9,... | collective-permute-start | bytes 786440 | tf_op jit(solution)/shard_map/ppermute | solution.py:12
  515.5 33.3 %collective-permute-start.27 = (f32[128,512]{0,1:T(8,128)S(1)}, f32[128,512]{0,1:T(8,128)S(1)}, u32[]{:S(2)}, u32[]{:S(2)}) collective-permute-start(f32[128,512]{0,1:T(8,128)S(1)} %add.189), channel_id=1, source_target_pairs={{0,64},{1,65},{2,66},{3,67},{4,68},{5,69},{6,70},{7,71},{8,72},{9,... | collective-permute-start | bytes 786440 | tf_op jit(solution)/shard_map/ppermute | solution.py:12
  574.8 3.5 collective-permute-start.28
  578.3 8.0 collective-permute-start.29
  586.3 8.6 %collective-permute-start.30 = (f32[128,384]{0,1:T(8,128)S(1)}, f32[128,384]{0,1:T(8,128)S(1)}, u32[]{:S(2)}, u32[]{:S(2)}) collective-permute-start(f32[128,384]{0,1:T(8,128)S(1)} %add.191), channel_id=1, source_target_pairs={{0,4},{1,5},{2,6},{3,7},{4,0},{5,1},{6,2},{7,3},{8,12},{9,13},{10,... | collective-permute-start | bytes 589832 | tf_op jit(solution)/shard_map/ppermute | solution.py:12
  594.9 6.4 collective-permute-start.31
  601.4 12.1 %collective-permute-start.32 = (f32[128,384]{0,1:T(8,128)S(1)}, f32[128,384]{0,1:T(8,128)S(1)}, u32[]{:S(2)}, u32[]{:S(2)}) collective-permute-start(f32[128,384]{0,1:T(8,128)S(1)} %add.193), channel_id=1, source_target_pairs={{0,16},{1,17},{2,18},{3,19},{4,20},{5,21},{6,22},{7,23},{8,24},{9,... | collective-permute-start | bytes 589832 | tf_op jit(solution)/shard_map/ppermute | solution.py:12
  613.5 22.1 %collective-permute-start.33 = (f32[128,384]{0,1:T(8,128)S(1)}, f32[128,384]{0,1:T(8,128)S(1)}, u32[]{:S(2)}, u32[]{:S(2)}) collective-permute-start(f32[128,384]{0,1:T(8,128)S(1)} %add.194), channel_id=1, source_target_pairs={{0,32},{1,33},{2,34},{3,35},{4,36},{5,37},{6,38},{7,39},{8,40},{9,... | collective-permute-start | bytes 589832 | tf_op jit(solution)/shard_map/ppermute | solution.py:12
  635.7 26.4 %collective-permute-start.34 = (f32[128,384]{0,1:T(8,128)S(1)}, f32[128,384]{0,1:T(8,128)S(1)}, u32[]{:S(2)}, u32[]{:S(2)}) collective-permute-start(f32[128,384]{0,1:T(8,128)S(1)} %add.195), channel_id=1, source_target_pairs={{0,64},{1,65},{2,66},{3,67},{4,68},{5,69},{6,70},{7,71},{8,72},{9,... | collective-permute-start | bytes 589832 | tf_op jit(solution)/shard_map/ppermute | solution.py:12
  662.1 7.9 collective-permute-start.35
  695.5 4.2 collective-permute-start.36
  699.8 6.6 collective-permute-start.37
  706.4 7.2 collective-permute-start.38
  713.7 5.7 collective-permute-start.39
  719.4 7.7 collective-permute-start.40
  727.1 18.3 %collective-permute-start.41 = (f32[128,256]{0,1:T(8,128)S(1)}, f32[128,256]{0,1:T(8,128)S(1)}, u32[]{:S(2)}, u32[]{:S(2)}) collective-permute-start(f32[128,256]{0,1:T(8,128)S(1)} %add.201), channel_id=1, source_target_pairs={{0,32},{1,33},{2,34},{3,35},{4,36},{5,37},{6,38},{7,39},{8,40},{9,... | collective-permute-start | bytes 393224 | tf_op jit(solution)/shard_map/ppermute | solution.py:12
  745.5 18.1 %collective-permute-start.42 = (f32[128,256]{0,1:T(8,128)S(1)}, f32[128,256]{0,1:T(8,128)S(1)}, u32[]{:S(2)}, u32[]{:S(2)}) collective-permute-start(f32[128,256]{0,1:T(8,128)S(1)} %add.202), channel_id=1, source_target_pairs={{0,64},{1,65},{2,66},{3,67},{4,68},{5,69},{6,70},{7,71},{8,72},{9,... | collective-permute-start | bytes 393224 | tf_op jit(solution)/shard_map/ppermute | solution.py:12
  763.6 6.5 collective-permute-start.43
  770.1 7.2 collective-permute-start.44
where the time goes:
time: 809 us; the launch traced here: 803 us
  waiting for transfers between devices  397 us (49%)
  other arithmetic  207 us (26%)
  starting transfers between devices  150 us (19%)
  matrix products  41.5 us (5%)
    ppermute x45, waiting for transfers between devices, swapped(): return lax.ppermute(value, axis, pairs)  397 us
    ppermute x45, starting transfers between devices, swapped(): return lax.ppermute(value, axis, pairs)  150 us
    another operation x27, other arithmetic, core_solve(): factor = jnp.linalg.cholesky(normal)  111 us
    another operation x18, other arithmetic, core_solve(): jax.scipy.linalg.cho_solve((factor, True), jnp.dot(system.T, right_part,...  94.2 us
  transfers between devices with their start and end apart: 45, of which 45 were waited for; matrix products, arithmetic and copies ran while one was open for 0% of the time, Pallas kernels for 0%

commit v1 on v0

v1 whole, which is shorter than its diff:
```python
import functools

import jax
import jax.numpy as jnp
from jax import lax
from jax.experimental import pallas as pl
from jax.experimental.pallas import tpu as pltpu
from jax.sharding import PartitionSpec as P

F32 = jnp.float32
RANK = 128
PARTNERS = ((0,), (1,), (1, 2), (3,), (4,), (5,), (5, 6), (7,), (7, 8))
RING = ((1,), (2,), (1, 2))
CORE = (0,)


def dot(a, b):
    return jnp.dot(a, b, precision=lax.Precision.HIGH, preferred_element_type=F32)


def dot6(a, b):
    return jnp.dot(a, b, precision=lax.Precision.HIGHEST, preferred_element_type=F32)


def bit(index, b):
    return lax.rem(lax.div(index, 2**b), 2)


def flipped(index, bits):
    for b in bits:
        index = index + (1 - 2 * bit(index, b)) * 2**b
    return index


def chebyshev_heights(count, at):
    heights = [at]
    for _ in range(count):
        heights.append(2 * heights[-1] ** 2 - 1)
    return heights


def inverse(g_own, g_other, midway):
    rows = lax.broadcasted_iota(jnp.int32, (RANK, RANK), 0)
    cols = lax.broadcasted_iota(jnp.int32, (RANK, RANK), 1)
    eye = jnp.where(rows == cols, 1.0, 0.0).astype(F32)
    system = eye - dot6(g_other, g_own)
    system_t = eye - dot6(g_own, g_other)
    normal = dot6(system_t, system)
    heights = chebyshev_heights(5, 1.25)
    poly = 1.25 * eye - normal
    result = system_t
    scale = 1.0 / heights[5]
    for step in range(5):
        if step == 2:
            midway()
        result = dot6(eye + poly * (1.0 / heights[step]), result)
        scale = scale * 2 * heights[step]
        if step < 4:
            poly = 2.0 * dot6(poly, poly) - eye
    return result * scale


def kernel(levels, n_sems, right_ref, inv_ref, bases_ref, out_ref, work, *scratch):
    def width(level):
        return (levels + 2 - level) * RANK

    def slice_rows(level):
        return RANK // min(2 ** (level - 1), 8)

    scratch = list(scratch)
    own, other, total = {}, {}, {}
    mine, theirs, coef, turned = {}, {}, {}, {}
    for level in range(1, levels + 1):
        own[level] = scratch.pop(0)
        other[level] = scratch.pop(0)
        if level < levels:
            coef[level] = scratch.pop(0)
            turned[level] = scratch.pop(0)
            total[level] = scratch.pop(0)
        for row in range(level + 1, levels + 1):
            mine[level, row] = scratch.pop(0)
            theirs[level, row] = scratch.pop(0)
    send_sem, recv_sem = scratch

    me = lax.axis_index("leaf")
    core = bit(me, 0)
    low_split = lax.rem(bit(me, 1) + bit(me, 2), 2)
    high_split = bit(me, 2)
    offsets = {1: 0, 2: 64 * core, 3: 64 * core + 32 * low_split}
    after = 64 * core + 32 * low_split + 16 * high_split

    def offset(level):
        return offsets.get(level, after)

    def partner_part(level):
        return {1: 64 * (1 - core), 2: 32 * (1 - low_split), 3: 16 * (1 - high_split)}.get(level, 0)

    def own_part(level):
        return {1: 64 * core, 2: 32 * low_split, 3: 16 * high_split}.get(level, 0)

    def rows_at(start, size):
        return pl.ds(start if isinstance(start, int) else pl.multiple_of(start, 16), size)

    count = [0]
    pending = []

    def send(src, dst, bits):
        k = count[0]
        count[0] += 1
        copy = pltpu.make_async_remote_copy(
            src_ref=src,
            dst_ref=dst,
            send_sem=send_sem.at[k],
            recv_sem=recv_sem.at[k],
            device_id=(flipped(me, bits),),
            device_id_type=pl.DeviceIdType.MESH,
        )
        copy.start()
        pending.append(copy)
        return copy

    partners = set(PARTNERS[:levels])
    if levels >= 3:
        partners |= set(RING)
    partners = sorted(partners | {CORE})
    barrier = pltpu.get_barrier_semaphore()
    for bits in partners:
        pl.semaphore_signal(
            barrier, inc=1, device_id=(flipped(me, bits),), device_id_type=pl.DeviceIdType.MESH
        )

    work[:, :RANK] = dot(inv_ref[...], right_ref[...])
    for level in range(levels, 0, -1):
        at = (levels + 1 - level) * RANK
        work[:, at : at + RANK] = dot(inv_ref[...], bases_ref[level - 1])
    own[1][...] = dot(bases_ref[0].T, work[...])
    for row in range(2, levels + 1):
        mine[1, row][...] = dot(bases_ref[row - 1].T, work[:, : width(row)])

    pl.semaphore_wait(barrier, len(partners))

    def start_gather(ref, level, cols):
        here = ref.at[rows_at(offset(level), slice_rows(level)), cols]
        ring = {2: (), 3: ((1,),)}.get(level, RING)
        return [send(here, here, bits) for bits in ring]

    def forward(ref, cols, copies):
        for copy in copies:
            copy.wait_recv()
        here = ref.at[rows_at(64 * core, 64), cols]
        return send(here, here, CORE)

    for level in range(1, levels + 1):
        bits = PARTNERS[level - 1]
        rest = width(level) - RANK
        wide, narrow = slice(rest, rest + RANK), slice(0, rest)
        size, next_size = slice_rows(level), slice_rows(level + 1)
        last = level == levels
        a_ref, b_ref = own[level], other[level]
        settled = list(pending)
        pending.clear()

        here = rows_at(offset(level), size)
        got_g = send(a_ref.at[here, wide], b_ref.at[here, wide], bits)
        got_rest = send(a_ref.at[here, narrow], b_ref.at[here, narrow], bits)
        got_rows = {}
        for row in range(level + 1, levels + 1):
            src = mine[level, row]
            if row > level + 1 and next_size < size:
                src = src.at[rows_at(partner_part(level), next_size)]
            got_rows[row] = send(src, theirs[level, row], bits)

        if level > 1:
            old = width(level)
            work[:, :old] = work[:, :old] - dot(work[:, old : old + RANK], coef[level - 1][:RANK])
        for copy in settled:
            copy.wait_send()
        if not last:
            for row in range(level + 1, levels + 1):
                at = (levels + 1 - row) * RANK
                turned[level][at - RANK : at, :RANK] = a_ref[:, at : at + RANK].T

        def add_next():
            got_rows[level + 1].wait_recv()
            total[level][here] = mine[level, level + 1][...] + theirs[level, level + 1][...]

        got_g.wait_recv()
        if level == 1:
            got_rest.wait_recv()
            if not last:
                add_next()
            x = inverse(a_ref[:, wide], b_ref[:, wide], lambda: None)
        else:
            ring_g = start_gather(b_ref, level, wide)
            got_rest.wait_recv()
            ring_rest = start_gather(b_ref, level, narrow)
            if not last:
                add_next()
                ring_total = start_gather(total[level], level, slice(None))
            core_g = forward(b_ref, wide, ring_g)
            core_rest = forward(b_ref, narrow, ring_rest)
            core_total = []
            core_g.wait_recv()

            def midway():
                if not last:
                    core_total.append(forward(total[level], slice(None), ring_total))

            x = inverse(a_ref[:, wide], b_ref[:, wide], midway)
            core_rest.wait_recv()

        a_rest, b_rest = a_ref[:, narrow], b_ref[:, narrow]
        coef_own = dot(x, b_rest - dot(b_ref[:, wide], a_rest))
        if last:
            out_ref[...] = work[:, :RANK] - dot(work[:, RANK : 2 * RANK], coef_own)
            break
        coef[level][:RANK] = coef_own
        coef[level][RANK:] = dot(x.T, a_rest - dot(a_ref[:, wide], b_rest))
        for row in range(level + 1, levels + 1):
            at = (levels + 1 - row) * RANK
            turned[level][at - RANK : at, RANK:] = b_ref[:, at : at + RANK].T
        if level > 1:
            core_total[0].wait_recv()
        own[level + 1][...] = total[level][...] - dot(
            turned[level][rest - 2 * RANK : rest - RANK, :], coef[level][...]
        )
        later = list(range(level + 2, levels + 1))
        if later:
            left = []
            for row in later:
                at = (levels - row) * RANK
                left.append(turned[level][rows_at(at + offset(level + 1), next_size), :])
            change = dot(jnp.concatenate(left, axis=0), coef[level][:, : width(level + 2)])
            for i, row in enumerate(later):
                got_rows[row].wait_recv()
                kept = mine[level, row][rows_at(own_part(level), next_size), :]
                mine[level + 1, row][...] = (
                    kept
                    + theirs[level, row][...]
                    - change[i * next_size : (i + 1) * next_size, : width(row)]
                )

    for copy in pending:
        copy.wait_send()
    assert count[0] == n_sems, count[0]


def n_copies(levels):
    total = 0
    for level in range(1, levels + 1):
        total += 2 + levels - level
        if level > 1:
            parts = 2 if level == levels else 3
            total += parts * ({2: 0, 3: 1}.get(level, 3) + 1)
    return total


def shards(right_side, leaf_inverse, bases):
    levels = bases.shape[0]
    n_sems = n_copies(levels)

    def width(level):
        return (levels + 2 - level) * RANK

    def slice_rows(level):
        return RANK // min(2 ** (level - 1), 8)

    def buffer(rows, cols):
        return pltpu.VMEM((rows, cols), F32)

    scratch = [buffer(right_side.shape[0], width(1))]
    for level in range(1, levels + 1):
        scratch += [buffer(RANK, width(level))] * 2
        if level < levels:
            scratch.append(buffer(2 * RANK, width(level + 1)))
            scratch.append(buffer(width(level + 1) - RANK, 2 * RANK))
            scratch.append(buffer(RANK, width(level + 1)))
        for row in range(level + 1, levels + 1):
            size = slice_rows(level)
            scratch.append(buffer(size, width(row)))
            scratch.append(buffer(size if row == level + 1 else slice_rows(level + 1), width(row)))
    scratch += [pltpu.SemaphoreType.DMA((n_sems,))] * 2
    vmem = pl.BlockSpec(memory_space=pltpu.VMEM)
    return pl.pallas_call(
        functools.partial(kernel, levels, n_sems),
        out_shape=jax.ShapeDtypeStruct(right_side.shape, F32),
        in_specs=[vmem] * 3,
        out_specs=vmem,
        scratch_shapes=scratch,
        compiler_params=pltpu.CompilerParams(
            collective_id=0, has_side_effects=True, vmem_limit_bytes=48 * 2**20
        ),
        name="tree_solve",
    )(right_side, leaf_inverse, bases)


def solution(mesh):
    return jax.shard_map(
        shards,
        mesh=mesh,
        in_specs=(P("leaf", None), P("leaf", None), P(None, "leaf", None)),
        out_specs=P("leaf", None),
        check_vma=False,
    )
```

time: 809 us -> 143 us (0.18)
  waiting for transfers between devices: 397 us -> 0 us
  other arithmetic: 207 us -> 0 us
  starting transfers between devices: 150 us -> 0 us
  Pallas kernels: 0 us -> 138 us
  matrix products: 41.5 us -> 0 us
    ppermute x45 -> x0, waiting for transfers between devices: 397 us -> none  [swapped(): return lax.ppermute(value, axis, pairs)]
    another operation x45 -> x0, other arithmetic: 206 us -> none  [the longest x27 111 us: core_solve(): factor = jnp.linalg.cholesky(normal)]
    ppermute x45 -> x0, starting transfers between devices: 150 us -> none  [swapped(): return lax.ppermute(value, axis, pairs)]
    pallas_call x0 -> x1, Pallas kernels: none -> 138 us  [shards(): pl.pallas_call(functools.partial(kernel, levels, n_sems), out_shape=jax.S...]
    dot_general x55 -> x0, matrix products: 33.5 us -> none  [the longest x9 8.87 us: shards(): jnp.dot(level_basis.T, current, precision=HIGH, preferred_element_type=jn...]
  transfers between devices with their start and end apart: 45 -> 0, of which waited for: 45 -> 0; matrix products, arithmetic and copies ran while one was open for 0% -> 0% of each run, Pallas kernels for 0% -> 0%
where the time goes in v1:
time: 143 us; the launch traced here: 142 us
  Pallas kernels  138 us (97%)
  local copies, waits for them, and re-layouts  3.78 us (3%)
    pallas_call x1, Pallas kernels, shards(): pl.pallas_call(functools.partial(kernel, levels, n_sems), out_shape=jax.S...  138 us
    unnamed x7, local copies, waits for them, and re-layouts  3.78 us

profile of v1, /device:TPU:1, one launch (start us, length us, event | category | flops | bytes accessed | tf_op | source)
XLA Modules:
  0.0 142.0 jit_solution(8108393832365247742)
XLA Ops:
  0.0 0.0 copy-start
  0.0 1.3 copy-done
  1.3 0.0 copy-start.1
  1.3 0.9 copy-done.1
  2.2 0.0 copy-start.2
  2.2 0.9 copy-done.2
  3.1 138.2 %tree_solve.1 = f32[256,128]{1,0:T(8,128)S(1)} custom-call(f32[256,128]{1,0:T(8,128)S(1)} %copy-done.2, f32[256,256]{1,0:T(8,128)S(1)} %copy-done.1, f32[9,256,128]{2,1,0:T(8,128)S(1)} %copy-done), custom_call_target="tpu_custom_call" | custom-call | tf_op jit(solution)/shard_map/tree_solve/pallas_call | solution.py:284
  141.3 0.7 copy.5
Async XLA Ops:
  0.0 1.3 copy-start
  1.3 0.9 copy-start.1
  2.2 0.9 copy-start.2

commit v2 on v1

v2 whole, which is shorter than its diff:
```python
import functools

import jax
import jax.numpy as jnp
from jax import lax
from jax.experimental import pallas as pl
from jax.experimental.pallas import tpu as pltpu
from jax.sharding import PartitionSpec as P

F32 = jnp.float32
RANK = 128
PARTNERS = ((0,), (1,), (1, 2), (3,), (4,), (5,), (5, 6), (7,), (7, 8))
RING = ((1,), (2,), (1, 2))
CORE = (0,)
AROUND = ((1,), (1, 2), CORE, (0, 1), (0, 1, 2), (2,), (0, 2))
WIDE = 8
STRAIGHT = 6


def dot(a, b):
    return jnp.dot(a, b, precision=lax.Precision.HIGH, preferred_element_type=F32)


def dot6(a, b):
    return jnp.dot(a, b, precision=lax.Precision.HIGHEST, preferred_element_type=F32)


def bit(index, b):
    return lax.rem(lax.div(index, 2**b), 2)


def flipped(index, bits):
    for b in bits:
        index = index + (1 - 2 * bit(index, b)) * 2**b
    return index


def chebyshev_heights(count, at):
    heights = [at]
    for _ in range(count):
        heights.append(2 * heights[-1] ** 2 - 1)
    return heights


def inverse(g_own, g_other, hook):
    rows = lax.broadcasted_iota(jnp.int32, (RANK, RANK), 0)
    cols = lax.broadcasted_iota(jnp.int32, (RANK, RANK), 1)
    eye = jnp.where(rows == cols, 1.0, 0.0).astype(F32)
    system = eye - dot6(g_other, g_own)
    system_t = eye - dot6(g_own, g_other)
    normal = dot6(system_t, system)
    heights = chebyshev_heights(5, 1.25)
    poly = 1.25 * eye - normal
    result = system_t
    scale = 1.0 / heights[5]
    for step in range(5):
        hook(step)
        result = dot6(eye + poly * (1.0 / heights[step]), result)
        scale = scale * 2 * heights[step]
        if step < 4:
            poly = 2.0 * dot6(poly, poly) - eye
    return result * scale


def slice_rows(level):
    if level >= WIDE:
        return 64
    return RANK // min(2 ** (level - 1), 8)


def row_rows(level):
    return 64 if level == 3 else slice_rows(level)


def ring_of(level):
    if level == 2 or level >= WIDE:
        return ()
    return ((1,),) if level == 3 else RING


def around_of(level):
    if level == 2 or level >= WIDE:
        return (CORE,)
    return ((1,), CORE, (0, 1)) if level == 3 else AROUND


def straight(level, first):
    return level >= STRAIGHT or first or ring_of(level) == ()


def n_copies(levels):
    total = 0
    for level in range(1, levels + 1):
        total += 2 + levels - level
        if level > 1:
            for part in range(2 if level == levels else 3):
                if level == 3 and part < 2:
                    total += 1
                elif straight(level, part == 0):
                    total += len(around_of(level))
                else:
                    total += len(ring_of(level)) + 1
            if level == WIDE - 1:
                total += (levels - level - 1) * len(ring_of(level))
    return total


def kernel(levels, n_sems, right_hbm, inv_hbm, bases_hbm, out_ref, work, *scratch):
    def width(level):
        return (levels + 2 - level) * RANK

    scratch = list(scratch)
    right_ref, inv_ref, bases_ref = scratch[:3]
    del scratch[:3]
    own, other, total = {}, {}, {}
    mine, theirs, coef, turned, summed = {}, {}, {}, {}, {}
    for level in range(1, levels + 1):
        own[level] = scratch.pop(0)
        other[level] = scratch.pop(0)
        if level < levels:
            coef[level] = scratch.pop(0)
            turned[level] = scratch.pop(0)
            total[level] = scratch.pop(0)
        for row in range(level + 1, levels + 1):
            mine[level, row] = scratch.pop(0)
            theirs[level, row] = scratch.pop(0)
            if level == WIDE - 1 and row > level + 1:
                summed[row] = scratch.pop(0)
    load_sem, send_sem, recv_sem = scratch

    loads = []
    for k, (src, dst) in enumerate(
        (
            (inv_hbm, inv_ref),
            (bases_hbm.at[0], bases_ref.at[0]),
            (right_hbm, right_ref),
            (bases_hbm.at[pl.ds(1, levels - 1)], bases_ref.at[pl.ds(1, levels - 1)]),
        )
    ):
        loads.append(pltpu.make_async_copy(src, dst, load_sem.at[k]))
        loads[-1].start()

    me = lax.axis_index("leaf")
    core = bit(me, 0)
    low_split = lax.rem(bit(me, 1) + bit(me, 2), 2)
    high_split = bit(me, 2)
    half = 64 * core
    quarter = half + 32 * low_split
    eighth = quarter + 16 * high_split

    def offset(level):
        if level == 1:
            return 0
        if level == 2 or level >= WIDE:
            return half
        return quarter if level == 3 else eighth

    def partner_part(level):
        return {1: 64 * (1 - core), 2: 32 * (1 - low_split), 3: 16 * (1 - high_split)}[level]

    def own_part(level):
        return {1: 64 * core, 2: 32 * low_split, 3: 16 * high_split}[level]

    def rows_at(start, size):
        return pl.ds(start if isinstance(start, int) else pl.multiple_of(start, 16), size)

    count = [0]
    pending = []

    def send(src, dst, bits):
        nonlocal pending
        k = count[0]
        count[0] += 1
        copy = pltpu.make_async_remote_copy(
            src_ref=src,
            dst_ref=dst,
            send_sem=send_sem.at[k],
            recv_sem=recv_sem.at[k],
            device_id=(flipped(me, bits),),
            device_id_type=pl.DeviceIdType.MESH,
        )
        copy.start()
        pending.append(copy)
        return copy

    partners = set(PARTNERS[:levels]) | {CORE}
    for level in range(2, levels + 1):
        partners |= set(around_of(level))
    partners = sorted(partners)
    barrier = pltpu.get_barrier_semaphore()
    for bits in partners:
        pl.semaphore_signal(
            barrier, inc=1, device_id=(flipped(me, bits),), device_id_type=pl.DeviceIdType.MESH
        )

    def leaf_work(level):
        at = (levels + 1 - level) * RANK
        work[:, at : at + RANK] = dot(inv_ref[...], bases_ref[level - 1])

    loads[0].wait()
    loads[1].wait()
    leaf_work(1)
    top = width(1) - RANK
    own[1][:, top:] = dot(bases_ref[0].T, work[:, top:])

    pl.semaphore_wait(barrier, len(partners))

    def gather(ref, level, cols, first):
        if level == 3 and ref is other[3]:
            here = ref.at[rows_at(half, 64), cols]
            return (ref, cols, [send(here, here, CORE)], True)
        here = ref.at[rows_at(offset(level), slice_rows(level)), cols]
        whole = straight(level, first)
        copies = [send(here, here, bits) for bits in (around_of if whole else ring_of)(level)]
        return (ref, cols, copies, whole)

    def forward(started):
        ref, cols, copies, whole = started
        if whole:
            return started
        for copy in copies:
            copy.wait_recv()
        here = ref.at[rows_at(half, 64), cols]
        return (ref, cols, [send(here, here, CORE)], True)

    def finish(started):
        for copy in started[2]:
            copy.wait_recv()

    got_rows = {}

    def send_row(level, row):
        size, next_size = slice_rows(level), slice_rows(level + 1)
        src = mine[level, row]
        if row > level + 1 and next_size < size:
            src = src.at[rows_at(partner_part(level), next_size)]
        got_rows[level, row] = send(src, theirs[level, row], PARTNERS[level - 1])

    def update_rows(level, rows):
        if not rows:
            return
        before, size = level - 1, slice_rows(level)
        left = []
        for row in rows:
            at = (levels - row) * RANK
            left.append(turned[before][rows_at(at + offset(level), size), :])
        left = left[0] if len(left) == 1 else jnp.concatenate(left, axis=0)
        change = dot(left, coef[before][:, : width(rows[0])])
        for i, row in enumerate(rows):
            if row in summed and level == WIDE:
                base = summed[row][rows_at(half, 64), :]
            else:
                got_rows[before, row].wait_recv()
                base = mine[before, row]
                if size < slice_rows(before):
                    base = base.at[rows_at(own_part(before), size)]
                base = base[...] + theirs[before, row][...]
            mine[level, row][...] = base - change[i * size : (i + 1) * size, : width(row)]
            send_row(level, row)

    def leaf_rows(rows):
        for row in rows:
            mine[1, row][...] = dot(bases_ref[row - 1].T, work[:, : width(row)])
            send_row(1, row)

    sent = []
    for level in range(1, levels + 1):
        bits = PARTNERS[level - 1]
        rest = width(level) - RANK
        wide, narrow = slice(rest, rest + RANK), slice(0, rest)
        last = level == levels
        a_ref, b_ref = own[level], other[level]
        sent.append(pending)
        pending = []
        later = list(range(level + 2, levels + 1))
        following = [] if last else [level + 1]
        here = rows_at(offset(level), slice_rows(level))
        mid = rows_at(half if level == 3 else offset(level), row_rows(level))

        def send_part(cols):
            return send(a_ref.at[mid, cols], b_ref.at[mid, cols], bits)

        def turn(ref, at_col):
            for row in range(level + 1, levels + 1):
                at = (levels + 1 - row) * RANK
                turned[level][at - RANK : at, at_col : at_col + RANK] = ref[:, at : at + RANK].T

        def settle():
            old = width(level)
            work[:, :old] = work[:, :old] - dot(work[:, old : old + RANK], coef[level - 1][:RANK])
            turn(a_ref, 0)
            if level > 2:
                for copy in sent[level - 2]:
                    copy.wait_send()

        def add_next():
            got_rows[level, level + 1].wait_recv()
            total[level][here] = mine[level, level + 1][...] + theirs[level, level + 1][...]

        def gather_next():
            if last:
                return []
            add_next()
            return [gather(total[level], level, slice(None), False)]

        got_g = send_part(wide)
        if level == 1:
            for copy in loads[2:]:
                copy.wait()
            work[:, :RANK] = dot(inv_ref[...], right_ref[...])
            for row in range(levels, 1, -1):
                leaf_work(row)
            a_ref[:, narrow] = dot(bases_ref[0].T, work[:, narrow])
            got_rest = send_part(narrow)
            leaf_rows(following)
            got_g.wait_recv()
            x = inverse(a_ref[:, wide], b_ref[:, wide], lambda step: leaf_rows(later[step : step + 1]))
            leaf_rows(later[5:])
            turn(a_ref, 0)
            got_rest.wait_recv()
        elif level <= 3:
            if level == 2:
                got_rest = send_part(narrow)
            update_rows(level, following)
            if level == 3:
                got_rest = send_part(narrow)
            settle()
            if level == 2:
                update_rows(level, later)
            got_g.wait_recv()
            finish(gather(b_ref, level, wide, True))
            x = inverse(a_ref[:, wide], b_ref[:, wide], lambda step: None)
            if level == 2:
                got_rest.wait_recv()
                all_rest = gather(b_ref, level, narrow, False)
                all_total = gather_next()
            else:
                all_total = gather_next()
                got_rest.wait_recv()
                all_rest = gather(b_ref, level, narrow, False)
                all_total = [forward(part) for part in all_total]
                update_rows(level, later)
            finish(all_rest)
        else:
            got_rest = send_part(narrow)
            if level > 4:
                update_rows(level, following)
            settle()
            got_g.wait_recv()
            all_g = gather(b_ref, level, wide, True)
            got_rest.wait_recv()
            held = [gather(b_ref, level, narrow, False)]
            if level == 4:
                update_rows(level, following)
            update_rows(level, later)
            all_total = [] if level >= WIDE else gather_next()
            finish(all_g)

            def hook(step):
                if step == 2:
                    held[0] = forward(held[0])
                if step == 3 and level >= WIDE:
                    all_total.extend(gather_next())

            x = inverse(a_ref[:, wide], b_ref[:, wide], hook)
            all_total = [forward(part) for part in all_total]
            if level == WIDE - 1:
                spread = []
                for row in later:
                    got_rows[level, row].wait_recv()
                    summed[row][here] = mine[level, row][...] + theirs[level, row][...]
                    part = summed[row].at[here]
                    spread += [send(part, part, ring) for ring in ring_of(level)]
            finish(held[0])

        a_rest, b_rest = a_ref[:, narrow], b_ref[:, narrow]
        coef_own = dot(x, b_rest - dot(b_ref[:, wide], a_rest))
        if last:
            out_ref[...] = work[:, :RANK] - dot(work[:, RANK : 2 * RANK], coef_own)
            break
        coef[level][:RANK] = coef_own
        coef[level][RANK:] = dot(x.T, a_rest - dot(a_ref[:, wide], b_rest))
        turn(b_ref, RANK)
        if level == 1:
            add_next()
        for part in all_total if level > 1 else ():
            finish(part)
        own[level + 1][...] = total[level][...] - dot(
            turned[level][rest - 2 * RANK : rest - RANK, :], coef[level][...]
        )
        if level == WIDE - 1:
            for copy in spread:
                copy.wait_recv()

    for copy in sum(sent[-1:], []) + pending:
        copy.wait_send()
    assert count[0] == n_sems, count[0]


def shards(right_side, leaf_inverse, bases):
    levels = bases.shape[0]
    n_sems = n_copies(levels)

    def width(level):
        return (levels + 2 - level) * RANK

    def buffer(*shape):
        return pltpu.VMEM(shape, F32)

    scratch = [buffer(right_side.shape[0], width(1))]
    scratch += [buffer(*right_side.shape), buffer(*leaf_inverse.shape), buffer(*bases.shape)]
    for level in range(1, levels + 1):
        scratch += [buffer(RANK, width(level))] * 2
        if level < levels:
            scratch.append(buffer(2 * RANK, width(level + 1)))
            scratch.append(buffer(width(level + 1) - RANK, 2 * RANK))
            scratch.append(buffer(RANK, width(level + 1)))
        for row in range(level + 1, levels + 1):
            size, next_size = slice_rows(level), slice_rows(level + 1)
            scratch.append(buffer(size, width(row)))
            scratch.append(buffer(size if row == level + 1 else min(size, next_size), width(row)))
            if level == WIDE - 1 and row > level + 1:
                scratch.append(buffer(RANK, width(row)))
    scratch.append(pltpu.SemaphoreType.DMA((4,)))
    scratch += [pltpu.SemaphoreType.DMA((n_sems,))] * 2
    return pl.pallas_call(
        functools.partial(kernel, levels, n_sems),
        out_shape=jax.ShapeDtypeStruct(right_side.shape, F32),
        in_specs=[pl.BlockSpec(memory_space=pl.ANY)] * 3,
        out_specs=pl.BlockSpec(memory_space=pltpu.VMEM),
        scratch_shapes=scratch,
        compiler_params=pltpu.CompilerParams(
            collective_id=0, has_side_effects=True, vmem_limit_bytes=56 * 2**20
        ),
        name="tree_solve",
    )(right_side, leaf_inverse, bases)


def solution(mesh):
    return jax.shard_map(
        shards,
        mesh=mesh,
        in_specs=(P("leaf", None), P("leaf", None), P(None, "leaf", None)),
        out_specs=P("leaf", None),
        check_vma=False,
    )
```

time: 143 us -> 129 us (0.902)
  Pallas kernels: 138 us -> 127 us
  local copies, waits for them, and re-layouts: 3.78 us -> 1.57 us
    pallas_call x1, Pallas kernels: 138 us -> 127 us  [shards(): pl.pallas_call(functools.partial(kernel, levels, n_sems), out_shape=jax.S...]
    unnamed x7 -> x1, local copies, waits for them, and re-layouts: 3.78 us -> 1.57 us
where the time goes in v2:
time: 129 us; the launch traced here: 128 us
  Pallas kernels  127 us (98%)
  local copies, waits for them, and re-layouts  1.57 us (1%)
    pallas_call x1, Pallas kernels, shards(): pl.pallas_call(functools.partial(kernel, levels, n_sems), out_shape=jax.S...  127 us

profile of v2, /device:TPU:1, one launch (start us, length us, event | category | flops | bytes accessed | tf_op | source)
XLA Modules:
  0.0 128.5 jit_solution(8382581344868932806)
XLA Ops:
  0.0 126.9 %tree_solve.1 = f32[256,128]{1,0:T(8,128)} custom-call(f32[256,128]{1,0:T(8,128)} %right_hbm.1, f32[256,256]{1,0:T(8,128)} %inv_hbm.1, f32[9,256,128]{2,1,0:T(8,128)} %bases_hbm.1), custom_call_target="tpu_custom_call" | custom-call | tf_op jit(solution)/shard_map/tree_solve/pallas_call | solution.py:426
  126.9 1.6 %copy.5 = f32[256,128]{1,0:T(8,128)} copy(f32[256,128]{1,0:T(8,128)} %tree_solve.1) | data formatting | bytes 262144

commit v3 on v2

v3 whole, which is shorter than its diff:
```python
import functools

import jax
import jax.numpy as jnp
from jax import lax
from jax.experimental import pallas as pl
from jax.experimental.pallas import tpu as pltpu
from jax.sharding import PartitionSpec as P

F32 = jnp.float32
RANK = 128
PARTNERS = ((0,), (1,), (1, 2), (3,), (4,), (5,), (5, 6), (7,), (7, 8))
RING = ((1,), (2,), (1, 2))
CORE = (0,)
AROUND = ((1,), (1, 2), CORE, (0, 1), (0, 1, 2), (2,), (0, 2))
WIDE = 8
HALVED = (3, 4)
STRAIGHT = 6


def dot(a, b):
    return jnp.dot(a, b, precision=lax.Precision.HIGH, preferred_element_type=F32)


def bit(index, b):
    return lax.rem(lax.div(index, 2**b), 2)


def flipped(index, bits):
    for b in bits:
        index = index + (1 - 2 * bit(index, b)) * 2**b
    return index


def chebyshev_heights(count, at):
    heights = [at]
    for _ in range(count):
        heights.append(2 * heights[-1] ** 2 - 1)
    return heights


def inverse(g_own, g_other, hook):
    rows = lax.broadcasted_iota(jnp.int32, (RANK, RANK), 0)
    cols = lax.broadcasted_iota(jnp.int32, (RANK, RANK), 1)
    eye = jnp.where(rows == cols, 1.0, 0.0).astype(F32)
    q, q_t = dot(g_other, g_own), dot(g_own, g_other)
    normal = eye - q - q_t + dot(q_t, q)
    heights = chebyshev_heights(5, 1.25)
    scale = 1.0 / heights[5]
    for height in heights[:5]:
        scale = scale * 2 * height
    poly = eye - 0.8 * normal
    result = (eye - q_t) * scale
    for step in range(5):
        hook(step)
        if step == 4:
            return result + jnp.dot(poly, result, preferred_element_type=F32)
        result = result + dot(poly, result)
        part = 1.0 / heights[step + 1]
        poly = (1.0 + part) * dot(poly, poly) - part * eye


def slice_rows(level):
    if level >= WIDE:
        return 64
    return RANK // min(2 ** (level - 1), 8)


def ring_of(level):
    if level == 2 or level >= WIDE:
        return ()
    return ((1,),) if level == 3 else RING


def around_of(level):
    if level == 2 or level >= WIDE:
        return (CORE,)
    return ((1,), CORE, (0, 1)) if level == 3 else AROUND


def straight(level, first):
    return level >= STRAIGHT or first or ring_of(level) == ()


def n_copies(levels):
    total = 0
    for level in range(1, levels + 1):
        total += 2 + levels - level
        if level == 2:
            total += max(levels - 3, 0)
        if level > 1:
            for part in range(2 if level == levels else 3):
                if level in HALVED and part == 0:
                    total += 1
                elif level == 3 and part == 2:
                    total += len(RING) + 1
                elif straight(level, part == 0):
                    total += len(around_of(level))
                else:
                    total += len(ring_of(level)) + 1
            if level == WIDE - 1:
                total += (levels - level - 1) * len(ring_of(level))
    return total


def kernel(levels, n_sems, right_hbm, inv_hbm, bases_hbm, out_ref, work, *scratch):
    def width(level):
        return (levels + 2 - level) * RANK

    scratch = list(scratch)
    right_ref, inv_ref, bases_ref = scratch[:3]
    del scratch[:3]
    both, total = {}, {}
    mine, theirs, coef, turned, summed = {}, {}, {}, {}, {}
    early, relayed = {}, {}
    for level in range(1, levels + 1):
        both[level] = scratch.pop(0)
        if level < levels:
            coef[level] = scratch.pop(0)
            turned[level] = scratch.pop(0)
            total[level] = scratch.pop(0)
        for row in range(level + 1, levels + 1):
            mine[level, row] = scratch.pop(0)
            theirs[level, row] = scratch.pop(0)
            if level == 2 and row > 3:
                early[row], relayed[row] = scratch.pop(0), scratch.pop(0)
            if level == WIDE - 1 and row > level + 1:
                summed[row] = scratch.pop(0)
    core_ref, load_sem, send_sem, recv_sem = scratch

    loads = []
    for k, (src, dst) in enumerate(
        (
            (inv_hbm, inv_ref),
            (bases_hbm.at[pl.ds(0, 2)], bases_ref.at[pl.ds(0, 2)]),
            (right_hbm, right_ref),
            (bases_hbm.at[pl.ds(2, levels - 2)], bases_ref.at[pl.ds(2, levels - 2)]),
        )
    ):
        loads.append(pltpu.make_async_copy(src, dst, load_sem.at[k]))
        loads[-1].start()

    me = lax.axis_index("leaf")
    core = bit(me, 0)
    low_split = lax.rem(bit(me, 1) + bit(me, 2), 2)
    high_split = bit(me, 2)
    half = 64 * core
    quarter = half + 32 * low_split
    eighth = quarter + 16 * high_split

    def offset(level):
        if level == 1:
            return 0
        if level == 2 or level >= WIDE:
            return half
        return quarter if level == 3 else eighth

    def partner_part(level):
        return {1: 64 * (1 - core), 2: 32 * (1 - low_split), 3: 16 * (1 - high_split)}[level]

    def own_part(level):
        return {1: 64 * core, 2: 32 * low_split, 3: 16 * high_split}[level]

    def rows_at(start, size):
        return pl.ds(start if isinstance(start, int) else pl.multiple_of(start, 16), size)

    count = [0]
    pending = []

    def send(src, dst, bits):
        nonlocal pending
        k = count[0]
        count[0] += 1
        copy = pltpu.make_async_remote_copy(
            src_ref=src,
            dst_ref=dst,
            send_sem=send_sem.at[k],
            recv_sem=recv_sem.at[k],
            device_id=(flipped(me, bits),),
            device_id_type=pl.DeviceIdType.MESH,
        )
        copy.start()
        pending.append(copy)
        return copy

    partners = set(PARTNERS[:levels]) | {CORE}
    for level in range(2, levels + 1):
        partners |= set(around_of(level))
    partners = sorted(partners)
    barrier = pltpu.get_barrier_semaphore()
    for bits in partners:
        pl.semaphore_signal(
            barrier, inc=1, device_id=(flipped(me, bits),), device_id_type=pl.DeviceIdType.MESH
        )

    def leaf_work(level):
        at = (levels + 1 - level) * RANK
        work[:, at : at + RANK] = dot(inv_ref[...], bases_ref[level - 1])

    loads[0].wait()
    loads[1].wait()
    leaf_work(1)
    leaf_work(2)
    top = width(1) - 2 * RANK
    both[1][RANK:, top:] = dot(bases_ref[0].T, work[:, top:])

    pl.semaphore_wait(barrier, len(partners))

    def gather(ref, level, cols, first):
        ahead = level == 3 and ref is not both[3]
        whole = straight(level, first)
        here = rows_at(eighth, 16) if ahead else rows_at(offset(level), slice_rows(level))
        if first and level in HALVED:
            here = rows_at(half, 64)
            return (ref, cols, [send(ref.at[here, cols], ref.at[here, cols], CORE)], True)
        here = ref.at[here, cols]
        ring = RING if ahead else ring_of(level)
        copies = [send(here, here, bits) for bits in (around_of(level) if whole else ring)]
        return (ref, cols, copies, whole)

    def forward(started):
        ref, cols, copies, whole = started
        if whole:
            return started
        for copy in copies:
            copy.wait_recv()
        here = ref.at[rows_at(half, 64), cols]
        return (ref, cols, [send(here, here, CORE)], True)

    def finish(started):
        for copy in started[2]:
            copy.wait_recv()

    got_rows, got_early = {}, {}
    spread = []

    def send_row(level, row):
        size, next_size = slice_rows(level), slice_rows(level + 1)
        src = mine[level, row]
        if level == 2 and row > 3:
            part = rows_at(32 * (1 - low_split) + 16 * (1 - high_split), 16)
            got_early[row] = send(src.at[part], early[row], PARTNERS[2])
            return
        if (row > level + 1 or level == 3) and next_size < size:
            src = src.at[rows_at(partner_part(level), next_size)]
        got_rows[level, row] = send(src, theirs[level, row], PARTNERS[level - 1])

    def relay(rows):
        for row in rows:
            got_early[row].wait_recv()
            part = rows_at(32 * (1 - low_split) + 16 * high_split, 16)
            relayed[row][...] = mine[2, row][part, :] + early[row][...]
            got_rows[2, row] = send(relayed[row], theirs[2, row], PARTNERS[1])

    def update_rows(level, rows):
        if not rows:
            return
        before, size = level - 1, slice_rows(level)
        left = []
        for row in rows:
            at = (levels - row) * RANK
            left.append(turned[before][rows_at(at + offset(level), size), :])
        left = left[0] if len(left) == 1 else jnp.concatenate(left, axis=0)
        change = dot(left, coef[before][:, : width(rows[0])])
        for i, row in enumerate(rows):
            if row in summed and level == WIDE:
                while spread:
                    spread.pop().wait_recv()
                base = summed[row][rows_at(half, 64), :]
            else:
                base = mine[before, row]
                if size < slice_rows(before):
                    base = base.at[rows_at(own_part(before), size)]
                base = base[...]
                for node in {2: (), 3: (2, 3)}.get(before, (before,)):
                    got_rows[node, row].wait_recv()
                    base = base + theirs[node, row][...]
            mine[level, row][...] = base - change[i * size : (i + 1) * size, : width(row)]
            send_row(level, row)

    def leaf_rows(rows):
        for row in rows:
            mine[1, row][...] = dot(bases_ref[row - 1].T, work[:, : width(row)])
            send_row(1, row)

    sent = []
    for level in range(1, levels + 1):
        bits = PARTNERS[level - 1]
        last = level == levels
        g_at = width(level) - RANK
        rest = g_at if last or level in HALVED else g_at - RANK
        wide, narrow, g_cols = slice(rest, None), slice(0, rest), slice(g_at, None)
        ab = both[level]
        sent.append(pending)
        pending = []
        later = list(range(level + 2, levels + 1))
        following = [] if last else [level + 1]
        here = rows_at(offset(level), slice_rows(level))

        def send_part(cols):
            size, start = slice_rows(level), offset(level)
            if level in HALVED and cols is wide:
                size, start = 64, half
            return send(
                ab.at[rows_at(start + RANK, size), cols], ab.at[rows_at(start, size), cols], bits
            )

        def turn(node, rows, first, to):
            for row in rows:
                at = (levels + 1 - row) * RANK
                block = both[node][first : first + RANK, at : at + RANK]
                turned[node][at - RANK : at, to : to + RANK] = block.T

        def settle_coef():
            before = level - 1
            turn(before, range(level + 1, levels + 1), 0, RANK)
            coef[before][...] = dot(core_ref[...], both[before][:, : width(level)])

        def settle():
            old = width(level)
            work[:, :old] = work[:, :old] - dot(work[:, old : old + RANK], coef[level - 1][:RANK])
            turn(level, range(level + 1, levels + 1), RANK, 0)
            if level > 2:
                for copy in sent[level - 2]:
                    copy.wait_send()

        def add_next():
            got_rows[level, level + 1].wait_recv()
            if level == 3:
                got_rows[2, 4].wait_recv()
                kept = mine[3, 4][rows_at(own_part(3), 16), :] + theirs[2, 4][...]
                total[3][rows_at(eighth, 16)] = kept + theirs[3, 4][...]
                return
            total[level][here] = mine[level, level + 1][...] + theirs[level, level + 1][...]

        def gather_next():
            if last:
                return []
            add_next()
            return [gather(total[level], level, slice(None), False)]

        def solve(hooks):
            return inverse(
                ab[RANK:, g_cols], ab[:RANK, g_cols], lambda step: hooks.get(step, lambda: None)()
            )

        got_wide = send_part(wide)
        if level == 1:
            for copy in loads[2:]:
                copy.wait()
            work[:, :RANK] = dot(inv_ref[...], right_ref[...])
            for row in range(levels, 2, -1):
                leaf_work(row)
            ab[RANK:, narrow] = dot(bases_ref[0].T, work[:, narrow])
            got_rest = send_part(narrow)
            leaf_rows(following)
            got_wide.wait_recv()
            x = solve({2: lambda: leaf_rows(later[:1])})
            turn(level, range(2, levels + 1), RANK, 0)
        elif level == 2:
            got_rest = send_part(narrow)
            settle_coef()
            update_rows(level, following)
            got_wide.wait_recv()
            all_wide = gather(ab, level, wide, True)
            leaf_rows(later)
            settle()
            update_rows(level, later)
            finish(all_wide)
            x = solve({})
        else:
            got_rest = send_part(narrow)
            settle_coef()
            update_rows(level, following)
            got_wide.wait_recv()
            all_wide = gather(ab, level, wide, True)
            got_rest.wait_recv()
            held = [gather(ab, level, narrow, False)]
            settle()
            if level > 3:
                update_rows(level, later)
            all_total = [] if level >= WIDE else gather_next()
            if level == 3:
                update_rows(level, later)
            finish(all_wide)

            def pass_on():
                held[0] = forward(held[0])
                if last:
                    finish(held[0])

            hooks = {4 if level == 3 else 2: pass_on}
            if level >= WIDE:
                hooks[3] = lambda: all_total.extend(gather_next())
            x = solve(hooks)

        if last:
            right = ab[:RANK, narrow] - dot(ab[:RANK, g_cols], ab[RANK:, narrow])
            out_ref[...] = work[:, :RANK] - dot(work[:, RANK : 2 * RANK], dot(x, right))
            break

        x_t = x.T
        core_ref[:RANK, :RANK] = x
        core_ref[RANK:, RANK:] = x_t
        core_ref[:RANK, RANK:] = -dot(x, ab[:RANK, g_cols])
        core_ref[RANK:, :RANK] = -dot(x_t, ab[RANK:, g_cols])

        def left_side():
            turn(level, [level + 1], 0, RANK)
            return dot(turned[level][g_at - 2 * RANK : g_at - RANK, :], core_ref[...])

        if level not in HALVED:
            left = left_side()
        if level == 1:
            got_rest.wait_recv()
        elif level == 2:
            got_rest.wait_recv()
            all_rest = gather(ab, level, narrow, False)
            relay(later)
            all_total = gather_next()
            finish(all_rest)
        else:
            all_total = [forward(part) for part in all_total]
            if level == WIDE - 1:
                for row in later:
                    got_rows[level, row].wait_recv()
                    summed[row][here] = mine[level, row][...] + theirs[level, row][...]
                    part = summed[row].at[here]
                    spread += [send(part, part, ring) for ring in ring_of(level)]
            finish(held[0])
        if level in HALVED:
            left = left_side()
        change = dot(left, ab[:, : width(level + 1)])
        if level == 1:
            add_next()
        else:
            for part in all_total:
                finish(part)
        both[level + 1][RANK:, :] = total[level][...] - change

    for copy in sum(sent[-1:], []) + pending:
        copy.wait_send()
    assert count[0] == n_sems, count[0]


def shards(right_side, leaf_inverse, bases):
    levels = bases.shape[0]
    n_sems = n_copies(levels)

    def width(level):
        return (levels + 2 - level) * RANK

    def buffer(*shape):
        return pltpu.VMEM(shape, F32)

    scratch = [buffer(right_side.shape[0], width(1))]
    scratch += [buffer(*right_side.shape), buffer(*leaf_inverse.shape), buffer(*bases.shape)]
    for level in range(1, levels + 1):
        scratch.append(buffer(2 * RANK, width(level)))
        if level < levels:
            scratch.append(buffer(2 * RANK, width(level + 1)))
            scratch.append(buffer(width(level + 1) - RANK, 2 * RANK))
            scratch.append(buffer(RANK, width(level + 1)))
        for row in range(level + 1, levels + 1):
            size, next_size = slice_rows(level), slice_rows(level + 1)
            scratch.append(buffer(size, width(row)))
            full = row == level + 1 and level != 3
            size = 16 if level in (2, 3) and row > 3 else size if full else min(size, next_size)
            scratch.append(buffer(size, width(row)))
            if level == 2 and row > 3:
                scratch += [buffer(size, width(row))] * 2
            if level == WIDE - 1 and row > level + 1:
                scratch.append(buffer(RANK, width(row)))
    scratch.append(buffer(2 * RANK, 2 * RANK))
    scratch.append(pltpu.SemaphoreType.DMA((4,)))
    scratch += [pltpu.SemaphoreType.DMA((n_sems,))] * 2
    return pl.pallas_call(
        functools.partial(kernel, levels, n_sems),
        out_shape=jax.ShapeDtypeStruct(right_side.shape, F32),
        in_specs=[pl.BlockSpec(memory_space=pl.ANY)] * 3,
        out_specs=pl.BlockSpec(memory_space=pltpu.VMEM),
        scratch_shapes=scratch,
        compiler_params=pltpu.CompilerParams(
            collective_id=0, has_side_effects=True, vmem_limit_bytes=56 * 2**20
        ),
        name="tree_solve",
    )(right_side, leaf_inverse, bases)


def solution(mesh):
    return jax.shard_map(
        shards,
        mesh=mesh,
        in_specs=(P("leaf", None), P("leaf", None), P(None, "leaf", None)),
        out_specs=P("leaf", None),
        check_vma=False,
    )
```

time: 129 us -> 122 us (0.946)
  Pallas kernels: 127 us -> 120 us
    pallas_call x1, Pallas kernels: 127 us -> 120 us  [shards(): pl.pallas_call(functools.partial(kernel, levels, n_sems), out_shape=jax.S...]
where the time goes in v3:
time: 122 us
  Pallas kernels  120 us (98%)
  local copies, waits for them, and re-layouts  1.57 us (1%)
    pallas_call x1, Pallas kernels, shards(): pl.pallas_call(functools.partial(kernel, levels, n_sems), out_shape=jax.S...  120 us

profile of v3, /device:TPU:1, one launch (start us, length us, event | category | flops | bytes accessed | tf_op | source)
XLA Modules:
  0.0 121.7 jit_solution(5989063656582203389)
XLA Ops:
  0.0 120.1 %tree_solve.1 = f32[256,128]{1,0:T(8,128)} custom-call(f32[256,128]{1,0:T(8,128)} %right_hbm.1, f32[256,256]{1,0:T(8,128)} %inv_hbm.1, f32[9,256,128]{2,1,0:T(8,128)} %bases_hbm.1), custom_call_target="tpu_custom_call" | custom-call | tf_op jit(solution)/shard_map/tree_solve/pallas_call | solution.py:477
  120.2 1.6 %copy.5 = f32[256,128]{1,0:T(8,128)} copy(f32[256,128]{1,0:T(8,128)} %tree_solve.1) | data formatting | bytes 262144

commit v4 on v3

--- a/solution.py
+++ b/solution.py
@@ -10,12 +10,12 @@
 F32 = jnp.float32
 RANK = 128
 PARTNERS = ((0,), (1,), (1, 2), (3,), (4,), (5,), (5, 6), (7,), (7, 8))
-RING = ((1,), (2,), (1, 2))
+RING = ((2,), (1, 2), (1,))
 CORE = (0,)
-AROUND = ((1,), (1, 2), CORE, (0, 1), (0, 1, 2), (2,), (0, 2))
+AROUND = ((0, 2), (2,), (0, 1, 2), (1, 2), (0, 1), (1,), CORE)
 WIDE = 8
 HALVED = (3, 4)
-STRAIGHT = 6
+STRAIGHT = 8
 
 
 def dot(a, b):
@@ -39,25 +39,27 @@
     return heights
 
 
-def inverse(g_own, g_other, hook):
+def inverses(pairs, hook):
     rows = lax.broadcasted_iota(jnp.int32, (RANK, RANK), 0)
     cols = lax.broadcasted_iota(jnp.int32, (RANK, RANK), 1)
     eye = jnp.where(rows == cols, 1.0, 0.0).astype(F32)
-    q, q_t = dot(g_other, g_own), dot(g_own, g_other)
-    normal = eye - q - q_t + dot(q_t, q)
     heights = chebyshev_heights(5, 1.25)
     scale = 1.0 / heights[5]
     for height in heights[:5]:
         scale = scale * 2 * height
-    poly = eye - 0.8 * normal
-    result = (eye - q_t) * scale
-    for step in range(5):
+    qs = [(dot(g_other, g_own), dot(g_own, g_other)) for g_own, g_other in pairs]
+    polys = [eye - 0.8 * (eye - q - q_t + dot(q_t, q)) for q, q_t in qs]
+    results = [(eye - q_t) * scale for q, q_t in qs]
+    for step in range(4):
         hook(step)
-        if step == 4:
-            return result + jnp.dot(poly, result, preferred_element_type=F32)
-        result = result + dot(poly, result)
+        results = [result + dot(poly, result) for poly, result in zip(polys, results)]
         part = 1.0 / heights[step + 1]
-        poly = (1.0 + part) * dot(poly, poly) - part * eye
+        polys = [(1.0 + part) * dot(poly, poly) - part * eye for poly in polys]
+    hook(4)
+    return [
+        result + jnp.dot(poly, result, preferred_element_type=F32)
+        for poly, result in zip(polys, results)
+    ]
 
 
 def slice_rows(level):
@@ -85,6 +87,8 @@
 def n_copies(levels):
     total = 0
     for level in range(1, levels + 1):
+        if level == WIDE:
+            return total + 17
         total += 2 + levels - level
         if level == 2:
             total += max(levels - 3, 0)
@@ -126,7 +130,7 @@
                 early[row], relayed[row] = scratch.pop(0), scratch.pop(0)
             if level == WIDE - 1 and row > level + 1:
                 summed[row] = scratch.pop(0)
-    core_ref, load_sem, send_sem, recv_sem = scratch
+    core_ref, core_far, both_far, turned_far, total_far, nine_far, load_sem, send_sem, recv_sem = scratch
 
     loads = []
     for k, (src, dst) in enumerate(
@@ -186,7 +190,11 @@
     partners = set(PARTNERS[:levels]) | {CORE}
     for level in range(2, levels + 1):
         partners |= set(around_of(level))
-    partners = sorted(partners)
+    quarters = ()
+    if levels > WIDE:
+        near, far = PARTNERS[WIDE - 1 : WIDE + 1]
+        quarters = (near, far, tuple(sorted(set(near) ^ set(far))))
+    partners = sorted(partners | set(quarters))
     barrier = pltpu.get_barrier_semaphore()
     for bits in partners:
         pl.semaphore_signal(
@@ -232,11 +240,15 @@
             copy.wait_recv()
 
     got_rows, got_early = {}, {}
-    spread = []
+    spread, got_nine = [], []
 
     def send_row(level, row):
         size, next_size = slice_rows(level), slice_rows(level + 1)
         src = mine[level, row]
+        if level == WIDE:
+            for way, dst in zip(quarters, (theirs[level, row], nine_far.at[0], nine_far.at[1])):
+                got_nine.append(send(src, dst, way))
+            return
         if level == 2 and row > 3:
             part = rows_at(32 * (1 - low_split) + 16 * (1 - high_split), 16)
             got_early[row] = send(src.at[part], early[row], PARTNERS[2])
@@ -288,7 +300,7 @@
         bits = PARTNERS[level - 1]
         last = level == levels
         g_at = width(level) - RANK
-        rest = g_at if last or level in HALVED else g_at - RANK
+        rest = g_at if last or level in HALVED or level == WIDE else g_at - RANK
         wide, narrow, g_cols = slice(rest, None), slice(0, rest), slice(g_at, None)
         ab = both[level]
         sent.append(pending)
@@ -340,9 +352,86 @@
             return [gather(total[level], level, slice(None), False)]
 
         def solve(hooks):
-            return inverse(
-                ab[RANK:, g_cols], ab[:RANK, g_cols], lambda step: hooks.get(step, lambda: None)()
+            pairs = [(ab[RANK:, g_cols], ab[:RANK, g_cols])]
+            return inverses(pairs, lambda step: hooks.get(step, lambda: None)())[0]
+
+        def core_of(x, ref, into):
+            x_t = x.T
+            into[:RANK, :RANK] = x
+            into[RANK:, RANK:] = x_t
+            into[:RANK, RANK:] = -dot(x, ref[:RANK, g_cols])
+            into[RANK:, :RANK] = -dot(x_t, ref[RANK:, g_cols])
+
+        if level == WIDE:
+            def send_all(cols):
+                src = ab.at[rows_at(half + RANK, 64), cols]
+                return [
+                    send(src, ab.at[rows_at(half, 64), cols], quarters[0]),
+                    send(src, both_far.at[rows_at(half + RANK, 64), cols], quarters[1]),
+                    send(src, both_far.at[rows_at(half, 64), cols], quarters[2]),
+                ]
+
+            def share(copies, cols):
+                shared = []
+                spots = ((ab, half), (both_far, half + RANK), (both_far, half))
+                for copy, (ref, start) in zip(copies, spots):
+                    copy.wait_recv()
+                    part = ref.at[rows_at(start, 64), cols]
+                    shared.append(send(part, part, CORE))
+                return shared
+
+            got_wide = send_all(wide)
+            got_rest = send_all(narrow)
+            settle_coef()
+            update_rows(level, following)
+            core_wide = share(got_wide, wide)
+            settle()
+            core_rest = share(got_rest, narrow)
+            for copy in core_wide:
+                copy.wait_recv()
+            core_nine = []
+
+            def add_nine(step):
+                if step != 4:
+                    return
+                for copy in got_nine:
+                    copy.wait_recv()
+                part = rows_at(half, 64)
+                total[level][part] = mine[level, levels][...] + theirs[level, levels][...]
+                total_far[part] = nine_far[0] + nine_far[1]
+                for ref in (total[level], total_far):
+                    core_nine.append(send(ref.at[part], ref.at[part], CORE))
+
+            x, x_far = inverses(
+                [
+                    (ab[RANK:, g_cols], ab[:RANK, g_cols]),
+                    (both_far[RANK:, g_cols], both_far[:RANK, g_cols]),
+                ],
+                add_nine,
             )
+            core_of(x, ab, core_ref)
+            core_of(x_far, both_far, core_far)
+            for copy in core_rest:
+                copy.wait_recv()
+            turn(level, [levels], 0, RANK)
+            turned_far[:, :RANK] = both_far[RANK:, RANK : 2 * RANK].T
+            turned_far[:, RANK:] = both_far[:RANK, RANK : 2 * RANK].T
+            left = dot(turned[level][...], core_ref[...])
+            left_far = dot(turned_far[...], core_far[...])
+            change = dot(left, ab[:, : 2 * RANK])
+            change_far = dot(left_far, both_far[:, : 2 * RANK])
+            for copy in core_nine:
+                copy.wait_recv()
+            nine = total[level][...] - change
+            nine_other = total_far[...] - change_far
+            g_own, g_other = nine[:, RANK:], nine_other[:, RANK:]
+            (x,) = inverses([(g_own, g_other)], lambda step: None)
+            cols = 2 * RANK
+            coef_own = dot(core_ref[:RANK, :], ab[:, :cols])
+            after = work[:, :cols] - dot(work[:, cols : cols + RANK], coef_own)
+            right = nine_other[:, :RANK] - dot(g_other, nine[:, :RANK])
+            out_ref[...] = after[:, :RANK] - dot(after[:, RANK:], dot(x, right))
+            break
 
         got_wide = send_part(wide)
         if level == 1:
@@ -376,34 +465,32 @@
             all_wide = gather(ab, level, wide, True)
             got_rest.wait_recv()
             held = [gather(ab, level, narrow, False)]
-            settle()
             if level > 3:
                 update_rows(level, later)
-            all_total = [] if level >= WIDE else gather_next()
+            if level >= 6:
+                settle()
+            all_total = gather_next()
             if level == 3:
                 update_rows(level, later)
+            if level < 6:
+                settle()
             finish(all_wide)
 
             def pass_on():
                 held[0] = forward(held[0])
-                if last:
-                    finish(held[0])
-
-            hooks = {4 if level == 3 else 2: pass_on}
-            if level >= WIDE:
-                hooks[3] = lambda: all_total.extend(gather_next())
-            x = solve(hooks)
+
+            x = solve({} if level == 4 else {4 if level == 3 else 2: pass_on})
+            if level == 5:
+                all_total = [forward(part) for part in all_total]
 
         if last:
             right = ab[:RANK, narrow] - dot(ab[:RANK, g_cols], ab[RANK:, narrow])
             out_ref[...] = work[:, :RANK] - dot(work[:, RANK : 2 * RANK], dot(x, right))
             break
 
-        x_t = x.T
-        core_ref[:RANK, :RANK] = x
-        core_ref[RANK:, RANK:] = x_t
-        core_ref[:RANK, RANK:] = -dot(x, ab[:RANK, g_cols])
-        core_ref[RANK:, :RANK] = -dot(x_t, ab[RANK:, g_cols])
+        core_of(x, ab, core_ref)
+        if level == 4:
+            pass_on()
 
         def left_side():
             turn(level, [level + 1], 0, RANK)
@@ -471,7 +558,9 @@
                 scratch += [buffer(size, width(row))] * 2
             if level == WIDE - 1 and row > level + 1:
                 scratch.append(buffer(RANK, width(row)))
-    scratch.append(buffer(2 * RANK, 2 * RANK))
+    scratch += [buffer(2 * RANK, 2 * RANK)] * 2
+    scratch += [buffer(2 * RANK, 3 * RANK), buffer(RANK, 2 * RANK), buffer(RANK, 2 * RANK)]
+    scratch.append(buffer(2, 64, 2 * RANK))
     scratch.append(pltpu.SemaphoreType.DMA((4,)))
     scratch += [pltpu.SemaphoreType.DMA((n_sems,))] * 2
     return pl.pallas_call(

time: 122 us -> 117 us (0.959)
  Pallas kernels: 120 us -> 115 us
    pallas_call x1, Pallas kernels: 120 us -> 115 us  [shards(): pl.pallas_call(functools.partial(kernel, levels, n_sems), out_shape=jax.S...]
where the time goes in v4:
time: 117 us
  Pallas kernels  115 us (98%)
  local copies, waits for them, and re-layouts  1.57 us (1%)
    pallas_call x1, Pallas kernels, shards(): pl.pallas_call(functools.partial(kernel, levels, n_sems), out_shape=jax.S...  115 us

profile of v4, /device:TPU:1, one launch (start us, length us, event | category | flops | bytes accessed | tf_op | source)
XLA Modules:
  0.0 117.0 jit_solution(2851916576997130315)
XLA Ops:
  0.0 115.4 %tree_solve.1 = f32[256,128]{1,0:T(8,128)} custom-call(f32[256,128]{1,0:T(8,128)} %right_hbm.1, f32[256,256]{1,0:T(8,128)} %inv_hbm.1, f32[9,256,128]{2,1,0:T(8,128)} %bases_hbm.1), custom_call_target="tpu_custom_call" | custom-call | tf_op jit(solution)/shard_map/tree_solve/pallas_call | solution.py:566
  115.4 1.6 %copy.5 = f32[256,128]{1,0:T(8,128)} copy(f32[256,128]{1,0:T(8,128)} %tree_solve.1) | data formatting | bytes 262144

commit v5 on v4

--- a/solution.py
+++ b/solution.py
@@ -465,12 +465,12 @@
             all_wide = gather(ab, level, wide, True)
             got_rest.wait_recv()
             held = [gather(ab, level, narrow, False)]
-            if level > 3:
+            if level == 4:
                 update_rows(level, later)
             if level >= 6:
                 settle()
             all_total = gather_next()
-            if level == 3:
+            if level != 4:
                 update_rows(level, later)
             if level < 6:
                 settle()

time: 117 us -> 117 us (level)
  no operation moved by 1% of the time
where the time goes in v5:
time: 117 us
  Pallas kernels  115 us (98%)
  local copies, waits for them, and re-layouts  1.57 us (1%)
    pallas_call x1, Pallas kernels, shards(): pl.pallas_call(functools.partial(kernel, levels, n_sems), out_shape=jax.S...  115 us

profile of v5, /device:TPU:1, one launch (start us, length us, event | category | flops | bytes accessed | tf_op | source)
XLA Modules:
  0.0 116.8 jit_solution(8840777967823581511)
XLA Ops:
  0.0 115.2 %tree_solve.1 = f32[256,128]{1,0:T(8,128)} custom-call(f32[256,128]{1,0:T(8,128)} %right_hbm.1, f32[256,256]{1,0:T(8,128)} %inv_hbm.1, f32[9,256,128]{2,1,0:T(8,128)} %bases_hbm.1), custom_call_target="tpu_custom_call" | custom-call | tf_op jit(solution)/shard_map/tree_solve/pallas_call | solution.py:566
  115.2 1.6 %copy.5 = f32[256,128]{1,0:T(8,128)} copy(f32[256,128]{1,0:T(8,128)} %tree_solve.1) | data formatting | bytes 262144

commit v6 on v5

--- a/solution.py
+++ b/solution.py
@@ -91,7 +91,7 @@
             return total + 17
         total += 2 + levels - level
         if level == 2:
-            total += max(levels - 3, 0)
+            total += max(levels - 3, 0) + (2 if levels > 2 else 0)
         if level > 1:
             for part in range(2 if level == levels else 3):
                 if level in HALVED and part == 0:
@@ -240,7 +240,7 @@
             copy.wait_recv()
 
     got_rows, got_early = {}, {}
-    spread, got_nine = [], []
+    spread, got_nine, got_halves = [], [], []
 
     def send_row(level, row):
         size, next_size = slice_rows(level), slice_rows(level + 1)
@@ -248,6 +248,12 @@
         if level == WIDE:
             for way, dst in zip(quarters, (theirs[level, row], nine_far.at[0], nine_far.at[1])):
                 got_nine.append(send(src, dst, way))
+            return
+        if level == 2 and row == 3:
+            cut = width(row) // (2 * RANK) * RANK
+            for cols in (slice(0, cut), slice(cut, width(row))):
+                copy = send(src.at[:, cols], theirs[2, 3].at[:, cols], PARTNERS[1])
+                got_halves.append((cols, copy))
             return
         if level == 2 and row > 3:
             part = rows_at(32 * (1 - low_split) + 16 * (1 - high_split), 16)
@@ -348,6 +354,13 @@
         def gather_next():
             if last:
                 return []
+            if level == 2:
+                parts = []
+                for cols, copy in got_halves:
+                    copy.wait_recv()
+                    total[2][here, cols] = mine[2, 3][:, cols] + theirs[2, 3][:, cols]
+                    parts.append(gather(total[2], 2, cols, False))
+                return parts
             add_next()
             return [gather(total[level], level, slice(None), False)]
 

time: 117 us -> 117 us (level)
  no operation moved by 1% of the time
where the time goes in v6:
time: 117 us
  Pallas kernels  115 us (98%)
  local copies, waits for them, and re-layouts  1.57 us (1%)
    pallas_call x1, Pallas kernels, shards(): pl.pallas_call(functools.partial(kernel, levels, n_sems), out_shape=jax.S...  115 us

profile of v6, /device:TPU:1, one launch (start us, length us, event | category | flops | bytes accessed | tf_op | source)
XLA Modules:
  0.0 117.0 jit_solution(15985513858261606605)
XLA Ops:
  0.0 115.4 %tree_solve.1 = f32[256,128]{1,0:T(8,128)} custom-call(f32[256,128]{1,0:T(8,128)} %right_hbm.1, f32[256,256]{1,0:T(8,128)} %inv_hbm.1, f32[9,256,128]{2,1,0:T(8,128)} %bases_hbm.1), custom_call_target="tpu_custom_call" | custom-call | tf_op jit(solution)/shard_map/tree_solve/pallas_call | solution.py:579
  115.4 1.6 %copy.5 = f32[256,128]{1,0:T(8,128)} copy(f32[256,128]{1,0:T(8,128)} %tree_solve.1) | data formatting | bytes 262144
